TPU v7x, 32 devices: a whole 2x2x4 slice. The times are simulated.
32 devices in a mesh: dp: 2 (over core), seq: 4 (over z), head: 4 (over y, x).
Axes of the slice: x: 2, y: 2, z: 4, core: 2. Of those that a mesh axis runs over, the one named last changes fastest.
Arguments:
- queries: bfloat16 [2, 2560, 2048], P('dp', ('seq', 'head')), may hold values from -45 to 45
- key_rows: bfloat16 [2, 2560, 2048], P('dp', ('seq', 'head')), may hold values from -6 to 6
- values: bfloat16 [2, 2560, 2048], P('dp', ('seq', 'head')), may hold values from -6 to 6
- rand_blocks: int32 [40, 16, 4], P('seq', 'head'), may hold values from 0 to 39, as said below
- out_weight: bfloat16 [2048, 2048], P('head'), may hold values from -0.125 to 0.125
- cotangent: bfloat16 [2, 2560, 2048], P('dp', ('seq', 'head')), may hold values from -6 to 6
Outputs:
- layer_out: bfloat16 [2, 2560, 2048], P('dp', ('seq', 'head'))
- grad_queries: bfloat16 [2, 2560, 2048], P('dp', ('seq', 'head'))
- grad_keys: bfloat16 [2, 2560, 2048], P('dp', ('seq', 'head'))
- grad_values: bfloat16 [2, 2560, 2048], P('dp', ('seq', 'head'))
- weight_grad: float32 [2048, 2048], P('head')
Inputs may be any that keep to these rules, and one draw needn't show every extreme that they name: `rand_blocks`: key block b lies in range b // 10 of seq. Over the 10 query blocks of one index of seq and the 4 heads of one index of head, at most 60 of the listed random blocks lie in any one range of seq; in every draw, for every index of head, some range of seq receives exactly 60 of them from every index of seq.
All inputs are finite; a program needn't handle non-finite values.
Results may differ from a plain program's by a relative error of at most 0.034.
Values may be sent and summed in bfloat16 or wider, within the bound.
A program may use at most 192 MiB of HBM per device.

v0:
```python
import math

import jax
import jax.numpy as jnp
from jax import lax
from jax.sharding import PartitionSpec as P

HEAD_SIZE = 128
BLOCK_TOKENS = 64


def with_halo(block, sides, width):
    for axis, dim in sides:
        count = lax.axis_size(axis)
        forward = [(i, i + 1) for i in range(count - 1)]
        backward = [(target, source) for source, target in forward]
        low = lax.ppermute(
            lax.slice_in_dim(block, block.shape[dim] - width, None, axis=dim), axis, forward
        )
        high = lax.ppermute(lax.slice_in_dim(block, 0, width, axis=dim), axis, backward)
        block = jnp.concatenate([low, block, high], axis=dim)
    return block


def from_root(block, axis, holder):
    block = jnp.where(lax.axis_index(axis) == holder, block, jnp.zeros_like(block))
    return lax.psum(block, axis)


def per_device(queries, key_rows, values, rand_blocks, out_weight, cotangent):
    block_len = BLOCK_TOKENS
    head_dim = HEAD_SIZE
    seq_count = lax.axis_size("seq")
    seq_index = lax.axis_index("seq")
    q_heads, k_heads, v_heads = (
        lax.all_to_all(queries, "head", split_axis=2, concat_axis=1, tiled=True),
        lax.all_to_all(key_rows, "head", split_axis=2, concat_axis=1, tiled=True),
        lax.all_to_all(values, "head", split_axis=2, concat_axis=1, tiled=True),
    )
    q_rows = q_heads[0]
    shard_len = q_rows.shape[0]
    width_cols = q_rows.shape[1]
    head_count = width_cols // head_dim
    block_count = shard_len // block_len
    rand_count = rand_blocks.shape[2]
    key_value = jnp.concatenate([k_heads[0], v_heads[0]], axis=1)
    padded = with_halo(key_value, (("seq", 0),), block_len)
    first_block = from_root(key_value[:block_len], "seq", 0)
    requests = jnp.transpose(rand_blocks, (0, 2, 1)).reshape(-1)
    request_count = requests.shape[0]
    head_of = jnp.arange(request_count, dtype=jnp.int32) % head_count
    capacity = 3 * request_count // (2 * seq_count)
    owners = requests // block_count
    offsets = requests % block_count
    one_hot = (owners[:, None] == jnp.arange(seq_count, dtype=jnp.int32)[None, :]).astype(jnp.int32)
    position = jnp.sum(one_hot * (jnp.cumsum(one_hot, axis=0) - 1), axis=1)
    slot_of = owners * capacity + position
    asked_codes = (
        jnp.full((seq_count * capacity,), -1, jnp.int32)
        .at[slot_of]
        .set(offsets * head_count + head_of)
        .reshape(seq_count, capacity)
    )
    asked_here = lax.all_to_all(asked_codes, "seq", split_axis=0, concat_axis=0, tiled=True)
    is_valid = asked_here >= 0
    asked_block = jnp.maximum(asked_here, 0) // head_count
    asked_head = jnp.maximum(asked_here, 0) % head_count
    block_view = key_value.reshape(block_count, block_len, 2, head_count, head_dim)
    served = block_view[asked_block, :, :, asked_head, :]
    served = jnp.where(is_valid[:, :, None, None, None], served, jnp.zeros_like(served))
    served = served.reshape(seq_count, capacity, block_len, 2 * head_dim)
    received = lax.all_to_all(served, "seq", split_axis=0, concat_axis=0, tiled=True)
    far_pairs = received.reshape(seq_count * capacity, block_len, 2, head_dim)[slot_of]
    pair_view = padded.reshape(block_count + 2, block_len, 2, head_count, head_dim)
    window_pairs = jnp.stack(
        [pair_view[:block_count], pair_view[1 : block_count + 1], pair_view[2:]], axis=1
    ).reshape(block_count, 3 * block_len, 2, head_count, head_dim)
    window_keys = window_pairs[:, :, 0]
    window_vals = window_pairs[:, :, 1]
    first_pairs = first_block.reshape(block_len, 2, head_count, head_dim)
    first_keys = first_pairs[:, 0]
    first_vals = first_pairs[:, 1]
    far_view = far_pairs.reshape(block_count, rand_count, head_count, block_len, 2, head_dim)
    far_keys = far_view[:, :, :, :, 0]
    far_vals = far_view[:, :, :, :, 1]
    global_ids = seq_index * block_count + jnp.arange(block_count, dtype=jnp.int32)
    block_total = seq_count * block_count
    window_live = jnp.stack([global_ids > 0, global_ids >= 0, global_ids < block_total - 1], axis=1)
    window_mask = jnp.repeat(window_live, block_len, axis=1)[None, :, None, :]
    query_blocks = q_rows.reshape(block_count, block_len, head_count, head_dim)
    softmax_scale = 1.0 / math.sqrt(head_dim)
    score_window = (
        jnp.einsum("ibhd,ikhd->hibk", query_blocks, window_keys, preferred_element_type=jnp.float32)
        * softmax_scale
    )
    score_first = (
        jnp.einsum("ibhd,khd->hibk", query_blocks, first_keys, preferred_element_type=jnp.float32)
        * softmax_scale
    )
    score_far = (
        jnp.einsum("ibhd,irhtd->hibrt", query_blocks, far_keys, preferred_element_type=jnp.float32)
        * softmax_scale
    )
    max_window = jnp.max(jnp.where(window_mask, score_window, -jnp.inf), axis=-1, keepdims=True)
    max_first = jnp.max(score_first, axis=-1, keepdims=True)
    max_far = jnp.max(score_far, axis=(-2, -1))[..., None]
    row_max = jnp.maximum(jnp.maximum(max_window, max_first), max_far)
    weight_window = jnp.where(window_mask, jnp.exp(score_window - row_max), 0.0)
    weight_first = jnp.exp(score_first - row_max)
    weight_far = jnp.exp(score_far - row_max[..., None])
    totals = (
        jnp.sum(weight_window, axis=-1, keepdims=True)
        + jnp.sum(weight_first, axis=-1, keepdims=True)
        + jnp.sum(weight_far, axis=(-2, -1))[..., None]
    )
    mixed = jnp.einsum(
        "hibk,ikhd->ibhd",
        weight_window.astype(jnp.bfloat16),
        window_vals,
        preferred_element_type=jnp.float32,
    )
    mixed = mixed + jnp.einsum(
        "hibk,khd->ibhd",
        weight_first.astype(jnp.bfloat16),
        first_vals,
        preferred_element_type=jnp.float32,
    )
    mixed = mixed + jnp.einsum(
        "hibrt,irhtd->ibhd",
        weight_far.astype(jnp.bfloat16),
        far_vals,
        preferred_element_type=jnp.float32,
    )
    totals_rows = jnp.transpose(totals, (1, 2, 0, 3))
    attn = (mixed / totals_rows).astype(jnp.bfloat16)
    logsum = row_max + jnp.log(totals)
    attn_rows = attn.reshape(shard_len, width_cols)
    layer_out = lax.psum_scatter(
        jnp.dot(attn_rows, out_weight, preferred_element_type=jnp.float32),
        "head",
        scatter_dimension=0,
        tiled=True,
    ).astype(jnp.bfloat16)[None]
    piece_flat = lax.all_gather(cotangent, "head", axis=1, tiled=True)[0]
    grad_piece = jnp.dot(piece_flat, out_weight.T, preferred_element_type=jnp.float32).astype(
        jnp.bfloat16
    )
    weight_acc = jnp.dot(attn_rows.T, piece_flat, preferred_element_type=jnp.float32)
    token_total = lax.axis_size("dp") * seq_count * shard_len
    weight_grad = lax.psum(weight_acc, ("dp", "seq")) * (1.0 / math.sqrt(token_total))
    grad_blocks = grad_piece.reshape(block_count, block_len, head_count, head_dim)
    delta_rows = jnp.sum(grad_blocks.astype(jnp.float32) * attn.astype(jnp.float32), axis=-1)
    row_delta = jnp.transpose(delta_rows, (2, 0, 1))[..., None]
    prob_window = jnp.where(window_mask, jnp.exp(score_window - logsum), 0.0)
    prob_first = jnp.exp(score_first - logsum)
    prob_far = jnp.exp(score_far - logsum[..., None])
    dprob_window = jnp.einsum(
        "ibhd,ikhd->hibk", grad_blocks, window_vals, preferred_element_type=jnp.float32
    )
    dprob_first = jnp.einsum(
        "ibhd,khd->hibk", grad_blocks, first_vals, preferred_element_type=jnp.float32
    )
    dprob_far = jnp.einsum(
        "ibhd,irhtd->hibrt", grad_blocks, far_vals, preferred_element_type=jnp.float32
    )
    dscore_window = (prob_window * (dprob_window - row_delta)).astype(jnp.bfloat16)
    dscore_first = (prob_first * (dprob_first - row_delta)).astype(jnp.bfloat16)
    dscore_far = (prob_far * (dprob_far - row_delta[..., None])).astype(jnp.bfloat16)
    grad_q = jnp.einsum(
        "hibk,ikhd->ibhd", dscore_window, window_keys, preferred_element_type=jnp.float32
    )
    grad_q = grad_q + jnp.einsum(
        "hibk,khd->ibhd", dscore_first, first_keys, preferred_element_type=jnp.float32
    )
    grad_q = grad_q + jnp.einsum(
        "hibrt,irhtd->ibhd", dscore_far, far_keys, preferred_element_type=jnp.float32
    )
    grad_q = (grad_q * softmax_scale).astype(jnp.bfloat16)
    key_window = (
        jnp.einsum(
            "hibk,ibhd->ikhd", dscore_window, query_blocks, preferred_element_type=jnp.float32
        )
        * softmax_scale
    )
    value_window = jnp.einsum(
        "hibk,ibhd->ikhd",
        prob_window.astype(jnp.bfloat16),
        grad_blocks,
        preferred_element_type=jnp.float32,
    )
    key_first = (
        jnp.einsum("hibk,ibhd->khd", dscore_first, query_blocks, preferred_element_type=jnp.float32)
        * softmax_scale
    )
    value_first = jnp.einsum(
        "hibk,ibhd->khd",
        prob_first.astype(jnp.bfloat16),
        grad_blocks,
        preferred_element_type=jnp.float32,
    )
    key_far = (
        jnp.einsum(
            "hibrt,ibhd->irhtd", dscore_far, query_blocks, preferred_element_type=jnp.float32
        )
        * softmax_scale
    )
    value_far = jnp.einsum(
        "hibrt,ibhd->irhtd",
        prob_far.astype(jnp.bfloat16),
        grad_blocks,
        preferred_element_type=jnp.float32,
    )
    window_terms = jnp.stack(
        [
            key_window.reshape(block_count, 3, block_len, head_count, head_dim),
            value_window.reshape(block_count, 3, block_len, head_count, head_dim),
        ],
        axis=3,
    )
    grad_pad = jnp.zeros((block_count + 2, block_len, 2, head_count, head_dim), jnp.float32)
    grad_pad = (
        grad_pad.at[:block_count]
        .add(window_terms[:, 0])
        .at[1 : block_count + 1]
        .add(window_terms[:, 1])
        .at[2:]
        .add(window_terms[:, 2])
    )
    global_grad = lax.psum(jnp.stack([key_first, value_first], axis=1), "seq")
    grad_pad = grad_pad.at[1].add(jnp.where(seq_index == 0, global_grad, 0.0))
    rims = jnp.concatenate([grad_pad[0], grad_pad[block_count + 1]], axis=0).reshape(
        2 * block_len, 2 * width_cols
    )
    rim_sums = with_halo(rims.astype(jnp.bfloat16), (("seq", 0),), block_len).astype(rims.dtype)
    core = grad_pad[1 : block_count + 1].reshape(shard_len, 2 * width_cols)
    core = (
        core.at[:block_len]
        .add(rim_sums[:block_len])
        .at[shard_len - block_len :]
        .add(rim_sums[3 * block_len :])
    )
    core = core.reshape(block_count, block_len, 2, head_count, head_dim)
    far_terms = (
        jnp.stack([key_far, value_far], axis=4)
        .reshape(request_count, block_len, 2, head_dim)
        .astype(jnp.bfloat16)
    )
    outgoing = (
        jnp.zeros((seq_count * capacity, block_len, 2, head_dim), jnp.bfloat16)
        .at[slot_of]
        .set(far_terms)
    )
    outgoing = outgoing.reshape(seq_count, capacity, block_len, 2 * head_dim)
    incoming = (
        lax.all_to_all(outgoing, "seq", split_axis=0, concat_axis=0, tiled=True)
        .reshape(seq_count, capacity, block_len, 2, head_dim)
        .astype(jnp.float32)
    )
    incoming = jnp.where(is_valid[:, :, None, None, None], incoming, 0.0)
    core = core.at[asked_block, :, :, asked_head, :].add(incoming)
    grad_k = core[:, :, 0].reshape(shard_len, width_cols).astype(jnp.bfloat16)
    grad_v = core[:, :, 1].reshape(shard_len, width_cols).astype(jnp.bfloat16)
    grad_q_rows = grad_q.reshape(shard_len, width_cols)
    grad_queries, grad_keys, grad_values = (
        lax.all_to_all(grad_q_rows[None], "head", split_axis=1, concat_axis=2, tiled=True),
        lax.all_to_all(grad_k[None], "head", split_axis=1, concat_axis=2, tiled=True),
        lax.all_to_all(grad_v[None], "head", split_axis=1, concat_axis=2, tiled=True),
    )
    return (layer_out, grad_queries, grad_keys, grad_values, weight_grad)


def solution(mesh):
    in_specs = (
        P("dp", ("seq", "head"), None),
        P("dp", ("seq", "head"), None),
        P("dp", ("seq", "head"), None),
        P("seq", "head", None),
        P("head", None),
        P("dp", ("seq", "head"), None),
    )
    out_specs = (
        P("dp", ("seq", "head"), None),
        P("dp", ("seq", "head"), None),
        P("dp", ("seq", "head"), None),
        P("dp", ("seq", "head"), None),
        P("head", None),
    )
    return jax.shard_map(
        per_device, mesh=mesh, in_specs=in_specs, out_specs=out_specs, check_vma=False
    )
```

profile of v0, /device:TPU:16, one launch (start us, length us, event | category | flops | bytes accessed | tf_op | source)
XLA Modules:
  0.0 901.4 jit_solution(3836464866967730779)
XLA Ops:
  14.1 5.2 all-to-all-start.3
  19.3 5.9 copy.315
  25.8 12.7 %reduce.14 = bf16[2048,160]{1,0:T(8,128)(2,1)S(1)} reduce(bf16[2048,1,160]{2,1,0:T(2,128)(2,1)} %bitcast.297, bf16[]{:T(256)} %broadcast.527), dimensions={1}, to_apply=%bitcast.255.reduce_sub_computation | reduce | bytes 1310722
  40.8 4.2 all-to-all-start.1
  45.0 5.9 copy.312
  50.9 12.7 %reduce.15 = bf16[2048,160]{1,0:T(8,128)(2,1)S(1)} reduce(bf16[2048,1,160]{2,1,0:T(2,128)(2,1)} %bitcast.301, bf16[]{:T(256)} %broadcast.527), dimensions={1}, to_apply=%bitcast.257.reduce_sub_computation | reduce | bytes 1310722
  65.9 4.5 all-to-all-start
  70.4 5.9 copy.320
  76.3 12.7 %reduce.13 = bf16[2048,160]{1,0:T(8,128)(2,1)S(1)} reduce(bf16[2048,1,160]{2,1,0:T(2,128)(2,1)} %bitcast.302, bf16[]{:T(256)} %broadcast.527), dimensions={1}, to_apply=%bitcast.259.reduce_sub_computation | reduce | bytes 1310722
  91.9 4.2 reshape.653
  96.1 4.5 copy.316
  101.3 4.2 all-to-all-start.2
  105.4 4.2 reshape.655
  109.7 5.7 copy.313
  117.6 3.4 collective-permute-start
  124.5 3.4 collective-permute-done.1
  127.9 5.5 pad_maximum_fusion.6
  137.8 12.2 %gather_fusion = bf16[240,64,2,128]{3,1,2,0:T(8,128)(2,1)} fusion(bf16[10,64,2,4,128]{4,1,3,2,0:T(8,128)(2,1)S(1)} %copy.335, s32[240]{0:T(256)S(1)} %reshape.602), kind=kCustom, calls=%fused_computation | custom fusion | bytes 15730560 | tf_op jit(solution)/shard_map/gather | solution.py:69
  150.0 15.3 %copy.336 = bf16[240,64,2,128]{3,2,1,0:T(2,128)(2,1)} copy(bf16[240,64,2,128]{3,1,2,0:T(8,128)(2,1)} %gather_fusion) | data formatting | bytes 15728640 | tf_op jit(solution)/shard_map/gather | solution.py:69
  165.4 13.4 %gather.9 = bf16[4,60,64,256]{3,2,1,0:T(8,128)(2,1)} reshape(bf16[240,64,2,128]{3,2,1,0:T(2,128)(2,1)} %copy.336) | data formatting | bytes 15728640 | tf_op jit(solution)/shard_map/gather | solution.py:69
  178.8 7.0 broadcast_select_fusion.1
  185.8 5.7 all-to-all-start.4
  193.2 4.2 reshape.657
  197.4 5.7 copy.321
  212.1 3.9 stack.41
  217.8 5.0 pad_maximum_fusion.1
  225.7 99.5 %all-reduce.6.cloned.1.call-done = bf16[64,2,4,128]{3,0,2,1:T(8,128)(2,1)} async-done(((bf16[64,2,4,128]{3,0,2,1:T(8,128)(2,1)}), bf16[64,2,4,128]{3,0,2,1:T(8,128)(2,1)}) %all-reduce.6.cloned.1.call-update) | async-done | bytes 131088 | tf_op jit(solution)/shard_map/psum | solution.py:27
  327.9 4.6 select_reduce_fusion
  334.8 4.1 fusion.66
  340.6 22.0 %all-to-all-done.4 = bf16[4,60,64,256]{3,2,1,0:T(8,128)(2,1)} async-done(((bf16[4,60,64,256]{3,2,1,0:T(8,128)(2,1)}), bf16[4,60,64,256]{3,2,1,0:T(8,128)(2,1)}, u32[]{:S(2)}, u32[]{:S(2)}) %all-to-all-start.4) | async-done | bytes 7864352 | tf_op jit(solution)/shard_map/all_to_all | solution.py:72
  362.6 11.9 %reshape.589 = bf16[240,64,2,128]{3,2,1,0:T(2,128)(2,1)} reshape(bf16[4,60,64,256]{3,2,1,0:T(8,128)(2,1)} %all-to-all-done.4) | data formatting | bytes 15728640 | tf_op jit(solution)/shard_map/reshape | solution.py:73
  374.5 8.5 copy.337
  383.1 11.2 %gather_fusion.1 = bf16[160,64,2,128]{3,1,2,0:T(8,128)(2,1)} fusion(bf16[240,64,2,128]{3,1,2,0:T(8,128)(2,1)} %copy.337, s32[1024]{0:T(1024)S(1)} %pad_clamp_fusion), kind=kCustom, calls=%fused_computation.1 | custom fusion | bytes 10486400 | tf_op jit(solution)/shard_map/gather | solution.py:73
  394.3 5.2 slice_bitcast_fusion.5
  421.2 4.9 broadcast_in_dim_reshape.5
  426.1 6.4 reduce.16
  435.5 4.3 all-to-all-start.5
  447.5 4.2 copy.383
  451.7 5.1 broadcast_in_dim.101
  456.7 24.1 %scatter_fusion = bf16[240,64,2,128]{3,1,2,0:T(8,128)(2,1)} fusion(bf16[240,64,2,128]{3,1,2,0:T(8,128)(2,1)} %broadcast_in_dim.101, s32[160]{0:T(256)S(1)} %bitcast.328, bf16[160,64,2,128]{3,1,2,0:T(8,128)(2,1)} %copy.383), kind=kCustom, calls=%fused_computation.3 | custom fusion | bytes 15729280 | tf_op jit(solution)/shard_map/scatter | solution.py:251
  480.8 15.3 %copy.384 = bf16[240,64,2,128]{3,2,1,0:T(2,128)(2,1)} copy(bf16[240,64,2,128]{3,1,2,0:T(8,128)(2,1)} %scatter_fusion) | data formatting | bytes 15728640 | tf_op jit(solution)/shard_map/scatter | solution.py:251
  496.2 13.4 %reshape.599 = bf16[4,60,64,256]{3,2,1,0:T(8,128)(2,1)} reshape(bf16[240,64,2,128]{3,2,1,0:T(2,128)(2,1)} %copy.384) | data formatting | bytes 15728640 | tf_op jit(solution)/shard_map/reshape | solution.py:253
  509.6 8.8 all-to-all-start.6
  523.5 5.8 fusion.17
  529.6 4.9 fusion.85
  540.9 3.8 fusion.14
  544.7 3.8 fusion.8
  548.5 109.6 %all-reduce.8.cloned.1.call-done = f32[64,2,4,128]{3,0,2,1:T(8,128)} async-done(((f32[64,2,4,128]{3,0,2,1:T(8,128)}), f32[64,2,4,128]{3,0,2,1:T(8,128)}) %all-reduce.8.cloned.1.call-update) | async-done | bytes 262160 | tf_op jit(solution)/shard_map/psum | solution.py:229
  670.5 3.2 copy.373
  673.7 4.1 reshape.596
  678.1 51.3 %collective-permute-done.3 = bf16[64,1024]{1,0:T(8,128)(2,1)S(1)} collective-permute-done((bf16[64,1024]{1,0:T(8,128)(2,1)S(1)}, bf16[64,1024]{1,0:T(8,128)(2,1)S(1)}, u32[]{:S(2)}, u32[]{:S(2)}) %collective-permute-start.3) | collective-permute-done | bytes 131104 | tf_op jit(solution)/shard_map/ppermute | solution.py:20
  733.6 4.2 reshape.598
  737.8 3.7 copy.385
  744.9 16.3 %reshape.601 = f32[4,60,64,2,128]{4,3,2,1,0:T(2,128)} reshape(bf16[4,60,64,256]{3,2,1,0:T(8,128)(2,1)} %all-to-all-done.6) | data formatting | bytes 23592960 | tf_op jit(solution)/shard_map/convert_element_type | solution.py:257
  761.2 12.2 %broadcast_select_fusion = f32[4,60,64,2,128]{4,3,2,1,0:T(2,128)} fusion(f32[4,60,64,2,128]{4,3,2,1,0:T(2,128)} %reshape.601, pred[4,60]{1,0:T(4,128)(4,1)S(1)} %bitcast.332), kind=kLoop, calls=%fused_computation.5 | loop fusion | flops 3932160 | bytes 31457520 | tf_op jit(solution)/shard_map/jit(_where)/select_n | solution.py:259
  773.4 13.4 %copy.386 = f32[240,64,2,128]{3,1,2,0:T(8,128)} copy(f32[240,64,2,128]{3,2,1,0:T(2,128)} %bitcast.282) | data formatting | bytes 31457280 | tf_op jit(solution)/shard_map/jit(_where)/select_n | solution.py:259
  786.8 50.9 %scatter_fusion.1 = f32[10,64,2,4,128]{4,1,3,2,0:T(8,128)} fusion(f32[10,64,2,4,128]{4,1,3,2,0:T(8,128)} %copy.385, s32[240]{0:T(256)S(1)} %reshape.632, f32[240,64,2,128]{3,1,2,0:T(8,128)} %copy.386), kind=kCustom, calls=%fused_computation.4 | custom fusion | flops 3932160 | bytes 47187840 | tf_op jit(solution)/shard_map/scatter-add | solution.py:260
  842.0 4.1 convert_element_type.101
  846.1 5.5 reduce.17
  854.5 6.0 all-to-all-start.7
  860.6 5.0 broadcast_multiply_fusion
  866.9 3.7 convert_element_type.102
  870.6 5.5 reduce.18
  879.1 4.2 all-to-all-start.8
  (195 shorter events, 133.8 us)
Async XLA Ops:
  8.0 326.8 %copy-start = (bf16[512,2048]{1,0:T(8,128)(2,1)S(1)}, bf16[512,2048]{1,0:T(8,128)(2,1)}, u32[]{:S(2)}) copy-start(bf16[512,2048]{1,0:T(8,128)(2,1)} %param.22) | copy-start | bytes 6291460
  14.1 26.7 %all-to-all-start.3 = ((s32[4,1,60]{2,1,0:T(1,128)}), s32[4,1,60]{2,1,0:T(1,128)S(1)}, u32[]{:S(2)}, u32[]{:S(2)}) async-start(s32[4,1,60]{2,1,0:T(1,128)} %all_to_all.93), calls=%async_computation.3 | async-start | bytes 4096 | tf_op jit(solution)/shard_map/all_to_all | solution.py:64
  40.8 25.1 %all-to-all-start.1 = ((bf16[4,2,40960]{2,1,0:T(2,128)(2,1)}), bf16[4,2,40960]{2,1,0:T(2,128)(2,1)}, u32[]{:S(2)}, u32[]{:S(2)}) async-start(bf16[4,2,40960]{2,1,0:T(2,128)(2,1)} %reshape.652), calls=%async_computation.1 | async-start | bytes 1310720 | tf_op jit(solution)/shard_map/all_to_all | solution.py:38
  65.9 35.3 %all-to-all-start = ((bf16[4,2,40960]{2,1,0:T(2,128)(2,1)}), bf16[4,2,40960]{2,1,0:T(2,128)(2,1)}, u32[]{:S(2)}, u32[]{:S(2)}) async-start(bf16[4,2,40960]{2,1,0:T(2,128)(2,1)} %reshape.654), calls=%async_computation | async-start | bytes 1310720 | tf_op jit(solution)/shard_map/all_to_all | solution.py:37
  101.2 16.4 %copy-start.12 = (bf16[1,4,160,512]{3,2,1,0:T(8,128)(2,1)}, bf16[1,4,160,512]{3,2,1,0:T(8,128)(2,1)S(1)}, u32[]{:S(2)}) copy-start(bf16[1,4,160,512]{3,2,1,0:T(8,128)(2,1)S(1)} %copy.317) | copy-start | bytes 1966084
  101.3 84.5 %all-to-all-start.2 = ((bf16[4,2,40960]{2,1,0:T(2,128)(2,1)}), bf16[4,2,40960]{2,1,0:T(2,128)(2,1)}, u32[]{:S(2)}, u32[]{:S(2)}) async-start(bf16[4,2,40960]{2,1,0:T(2,128)(2,1)} %reshape.656), calls=%async_computation.2 | async-start | bytes 1310720 | tf_op jit(solution)/shard_map/all_to_all | solution.py:36
  117.6 6.9 collective-permute-start
  121.0 6.9 collective-permute-start.1
  133.3 1.1 copy-start.5
  185.8 176.8 %all-to-all-start.4 = ((bf16[4,60,64,256]{3,2,1,0:T(8,128)(2,1)}), bf16[4,60,64,256]{3,2,1,0:T(8,128)(2,1)}, u32[]{:S(2)}, u32[]{:S(2)}) async-start(bf16[4,60,64,256]{3,2,1,0:T(8,128)(2,1)} %broadcast_select_fusion.1), calls=%async_computation.4 | async-start | bytes 15728640 | tf_op jit(solution)/shard_map/all_to_all | solution.py:72
  191.5 133.7 %all-reduce.6.cloned.1.call-start = ((), (), s32[]{:S(2)}) async-start(), calls=%async_computation.10 | async-start | bytes 262144 | tf_op jit(solution)/shard_map/psum | solution.py:27
  192.3 142.6 %all-gather.2.cloned.1.call-start = ((), (), s32[]{:S(2)}) async-start(), calls=%async_computation.12 | async-start | bytes 3276800 | tf_op jit(solution)/shard_map/all_gather | solution.py:144
  203.1 7.2 copy-start.6
  212.1 3.9 copy-start.13
  222.8 102.5 %copy-start.7 = (bf16[10,64,4,128]{3,2,1,0:T(4,128)(2,1)S(1)}, bf16[10,64,4,128]{3,2,1,0:T(4,128)(2,1)}, u32[]{:S(2)}) copy-start(bf16[10,64,4,128]{3,2,1,0:T(4,128)(2,1)} %reshape_squeeze.2) | copy-start | bytes 1966084
  327.9 4.6 copy-start.3
  400.4 1.7 copy-start.8
  401.9 1.4 copy-start.1
  408.2 1.0 copy-start.19
  408.2 1.6 copy-start.18
  409.8 2.3 copy-start.4
  414.1 4.9 copy-start.15
  415.9 1.5 copy-start.9
  417.4 1.6 copy-start.11
  418.2 0.8 copy-start.17
  435.5 74.1 %all-to-all-start.5 = ((bf16[4,2,40960]{2,1,0:T(2,128)(2,1)}), bf16[4,2,40960]{2,1,0:T(2,128)(2,1)}, u32[]{:S(2)}, u32[]{:S(2)}) async-start(bf16[4,2,40960]{2,1,0:T(2,128)(2,1)} %reshape.658), calls=%async_computation.6 | async-start | bytes 1310720 | tf_op jit(solution)/shard_map/all_to_all | solution.py:265
  443.6 1.7 copy-start.10
  509.6 235.3 %all-to-all-start.6 = ((bf16[4,60,64,256]{3,2,1,0:T(8,128)(2,1)}), bf16[4,60,64,256]{3,2,1,0:T(8,128)(2,1)}, u32[]{:S(2)}, u32[]{:S(2)}) async-start(bf16[4,60,64,256]{3,2,1,0:T(8,128)(2,1)} %reshape.599), calls=%async_computation.7 | async-start | bytes 15728640 | tf_op jit(solution)/shard_map/all_to_all | solution.py:255
  518.4 139.7 %all-reduce.8.cloned.1.call-start = ((), (), s32[]{:S(2)}) async-start(), calls=%async_computation.13 | async-start | bytes 524288 | tf_op jit(solution)/shard_map/psum | solution.py:229
  518.4 4.0 copy-start.2
  523.5 337.1 %all-reduce.10.cloned.1.call-start = ((), (), s32[]{:S(2)}) async-start(), calls=%async_computation.14 | async-start | bytes 8388608 | tf_op jit(solution)/shard_map/psum | solution.py:150
  529.4 353.9 %reduce-scatter.2.cloned.1.call-start = ((), (), s32[]{:S(2)}) async-start(), calls=%async_computation.11 | async-start | bytes 6553600 | tf_op jit(solution)/shard_map/reduce_scatter | solution.py:138
  534.6 2.2 copy-start.14
  659.8 8.5 copy-start.20
  662.3 67.1 %collective-permute-start.3 = (bf16[64,1024]{1,0:T(8,128)(2,1)S(1)}, bf16[64,1024]{1,0:T(8,128)(2,1)S(1)}, u32[]{:S(2)}, u32[]{:S(2)}) collective-permute-start(bf16[64,1024]{1,0:T(8,128)(2,1)S(1)} %concatenate.44), channel_id=1, source_target_pairs={{4,0},{8,4},{12,8},{5,1},{9,5},{13,9},{6,2},{10,6},{14,10},{7,3},{... | collective-permute-start | bytes 393224 | tf_op jit(solution)/shard_map/ppermute | solution.py:20
  665.6 65.6 %collective-permute-start.2 = (bf16[64,1024]{1,0:T(8,128)(2,1)S(1)}, bf16[64,1024]{1,0:T(8,128)(2,1)S(1)}, u32[]{:S(2)}, u32[]{:S(2)}) collective-permute-start(bf16[64,1024]{1,0:T(8,128)(2,1)S(1)} %concatenate.43), channel_id=1, source_target_pairs={{0,4},{4,8},{8,12},{1,5},{5,9},{9,13},{2,6},{6,10},{10,14},{3,7},{... | collective-permute-start | bytes 393224 | tf_op jit(solution)/shard_map/ppermute | solution.py:17
  854.5 24.5 %all-to-all-start.7 = ((bf16[4,2,40960]{2,1,0:T(2,128)(2,1)}), bf16[4,2,40960]{2,1,0:T(2,128)(2,1)}, u32[]{:S(2)}, u32[]{:S(2)}) async-start(bf16[4,2,40960]{2,1,0:T(2,128)(2,1)} %reshape.660), calls=%async_computation.8 | async-start | bytes 1310720 | tf_op jit(solution)/shard_map/all_to_all | solution.py:266
  860.5 5.1 copy-start.16
  879.1 11.6 %all-to-all-start.8 = ((bf16[4,2,40960]{2,1,0:T(2,128)(2,1)}), bf16[4,2,40960]{2,1,0:T(2,128)(2,1)}, u32[]{:S(2)}, u32[]{:S(2)}) async-start(bf16[4,2,40960]{2,1,0:T(2,128)(2,1)} %reshape.662), calls=%async_computation.9 | async-start | bytes 1310720 | tf_op jit(solution)/shard_map/all_to_all | solution.py:267
Sparse Core Ops, SparseCore 0:
  195.2 129.9 all-reduce.5
  523.6 134.4 all-reduce.7
  661.1 127.9 all-reduce.9
Sparse Core Ops, SparseCore 1:
  194.6 41.2 all-gather.1
  534.6 62.7 reduce-scatter.1
where the time goes:
time: 914 us; the launch traced here: 901 us
  local copies, waits for them, and re-layouts  323 us (35%)
  waiting for transfers between devices  290 us (32%)
  other arithmetic  173 us (19%)
  starting transfers between devices  59.8 us (7%)
  matrix products  39.3 us (4%)
  between operations  16.1 us (2%)
    psum x1, waiting for transfers between devices, per_device(): global_grad = lax.psum(jnp.stack([key_first, value_first], axis=1), 'seq')  110 us
    psum x1, waiting for transfers between devices, from_root(): return lax.psum(block, axis)  99.5 us
    unnamed x64, local copies, waits for them, and re-layouts  58.8 us
    unnamed x7, other arithmetic  55.6 us
    ppermute x2, waiting for transfers between devices, with_halo(): lax.ppermute(lax.slice_in_dim(block, 0, width, axis=dim), axis, backward)  54.7 us
    scatter-add x1, other arithmetic, per_device(): core = core.at[asked_block, :, :, asked_head, :].add(incoming)  50.9 us
    gather x3, local copies, waits for them, and re-layouts, per_device(): served = block_view[asked_block, :, :, asked_head, :]  40.9 us
    scatter x2, local copies, waits for them, and re-layouts, per_device(): outgoing = jnp.zeros((seq_count * capacity, block_len, 2, head_dim), jnp....  39.4 us
  transfers between devices with their start and end apart: 18, of which 8 were waited for; matrix products, arithmetic and copies ran while one was open for 49% of the time, Pallas kernels for 0%

commit v1 on v0

v1 whole, which is shorter than its diff:
```python
import functools
import math

import jax
import jax.numpy as jnp
from jax import lax
from jax.experimental import pallas as pl
from jax.experimental.pallas import tpu as pltpu
from jax.sharding import Mesh
from jax.sharding import PartitionSpec as P

HEAD_SIZE = 128
BLOCK_TOKENS = 64
SCALE = 1.0 / math.sqrt(HEAD_SIZE)
VMEM_LIMIT = 50 * 1024 * 1024
NEGATIVE = -1e30


def dot_nt(a, b):
    return lax.dot_general(a, b, (((1,), (1,)), ((), ())), preferred_element_type=jnp.float32)


def dot_nn(a, b):
    return lax.dot_general(a, b, (((1,), (0,)), ((), ())), preferred_element_type=jnp.float32)


def dot_tn(a, b):
    return lax.dot_general(a, b, (((0,), (0,)), ((), ())), preferred_element_type=jnp.float32)


def vmem():
    return pl.BlockSpec(memory_space=pltpu.VMEM)


def smem():
    return pl.BlockSpec(memory_space=pltpu.SMEM)


def column_of(chunk, lo_count, head_count):
    lo, h = chunk // head_count, chunk % head_count
    return (h * lo_count + lo) * HEAD_SIZE


def pack_kernel(lo_count, head_count, a_ref, b_ref, c_ref, out_ref):
    rows = a_ref.shape[0]
    for chunk in range(lo_count * head_count):
        col = column_of(chunk, lo_count, head_count)
        for j, ref in enumerate((a_ref, b_ref, c_ref)):
            out_ref[chunk, j * rows : (j + 1) * rows, :] = ref[:, col : col + HEAD_SIZE]


def unpack_kernel(lo_count, head_count, in_ref, a_ref, b_ref, c_ref):
    rows = a_ref.shape[0]
    for chunk in range(lo_count * head_count):
        col = column_of(chunk, lo_count, head_count)
        for j, ref in enumerate((a_ref, b_ref, c_ref)):
            ref[:, col : col + HEAD_SIZE] = in_ref[chunk, j * rows : (j + 1) * rows, :]


def load_chunks(packed_ref, dests):
    rows = packed_ref.shape[1] // 3

    def body(c, carry):
        at = pl.ds(pl.multiple_of(c * rows, rows), rows)
        for j, dest in enumerate(dests):
            if dest is not None:
                dest[at, :] = packed_ref[c, j * rows : (j + 1) * rows, :]
        return carry

    lax.fori_loop(0, packed_ref.shape[0], body, 0)


def block_at(ref, b):
    return ref[pl.ds(pl.multiple_of(b * BLOCK_TOKENS, BLOCK_TOKENS), BLOCK_TOKENS), :]


def slots_of(i, off_ref, idx_ref, rand_count, total):
    g = off_ref[0] + i
    ids = [jnp.maximum(g - 1, 0), g, jnp.minimum(g + 1, total - 1), jnp.int32(0)]
    ids += [idx_ref[i * rand_count + r] for r in range(rand_count)]
    return g, ids


def masked_scores(q, keys, g, total):
    s = dot_nt(q, keys) * SCALE
    col = lax.broadcasted_iota(jnp.int32, (1, keys.shape[0]), 1) // BLOCK_TOKENS
    dead = ((col == 0) & (g == 0)) | ((col == 2) & (g == total - 1))
    return jnp.where(dead, NEGATIVE, s)


def forward_kernel(
    rand_count, unroll, off_ref, idx_ref, packed_ref, attn_ref, q_s, k_s, v_s
):
    total = k_s.shape[0] // BLOCK_TOKENS
    load_chunks(packed_ref, (q_s, k_s, v_s))
    count = attn_ref.shape[0] // BLOCK_TOKENS

    def body(step, carry):
        results = []
        for u in range(unroll):
            i = step * unroll + u
            g, ids = slots_of(i, off_ref, idx_ref, rand_count, total)
            keys = jnp.concatenate([block_at(k_s, b) for b in ids], axis=0)
            vals = jnp.concatenate([block_at(v_s, b) for b in ids], axis=0)
            s = masked_scores(block_at(q_s, g), keys, g, total)
            e = jnp.exp(s - jnp.max(s, axis=-1, keepdims=True))
            l = jnp.sum(e, axis=-1, keepdims=True)
            results.append((i, (dot_nn(e.astype(jnp.bfloat16), vals) / l).astype(jnp.bfloat16)))
        for i, out in results:
            at = pl.ds(pl.multiple_of(i * BLOCK_TOKENS, BLOCK_TOKENS), BLOCK_TOKENS)
            attn_ref[at, :] = out
        return carry

    lax.fori_loop(0, count // unroll, body, 0)


def backward_kernel(
    rand_count, unroll, off_ref, idx_ref, packed_ref, attn_ref, grad_ref, out_ref,
    q_s, k_s, v_s, dq_s, dk_s, dv_s,
):
    total = k_s.shape[0] // BLOCK_TOKENS
    load_chunks(packed_ref, (q_s, k_s, v_s))
    dk_s[...] = jnp.zeros_like(dk_s)
    dv_s[...] = jnp.zeros_like(dv_s)
    count = attn_ref.shape[0] // BLOCK_TOKENS
    if count != total:
        dq_s[...] = jnp.zeros_like(dq_s)

    def body(step, carry):
        results = []
        for u in range(unroll):
            i = step * unroll + u
            g, ids = slots_of(i, off_ref, idx_ref, rand_count, total)
            keys = jnp.concatenate([block_at(k_s, b) for b in ids], axis=0)
            vals = jnp.concatenate([block_at(v_s, b) for b in ids], axis=0)
            q = block_at(q_s, g)
            do = block_at(grad_ref, i)
            attn = block_at(attn_ref, i)
            s = masked_scores(q, keys, g, total)
            e = jnp.exp(s - jnp.max(s, axis=-1, keepdims=True))
            p = e * (1.0 / jnp.sum(e, axis=-1, keepdims=True))
            dp = dot_nt(do, vals)
            delta = jnp.sum(
                do.astype(jnp.float32) * attn.astype(jnp.float32), axis=-1, keepdims=True
            )
            ds = (p * (dp - delta)).astype(jnp.bfloat16)
            dq = dot_nn(ds, keys) * SCALE
            dk = dot_tn(ds, q) * SCALE
            dv = dot_tn(p.astype(jnp.bfloat16), do)
            results.append((g, ids, dq, dk, dv))
        for g, ids, dq, dk, dv in results:
            at = pl.ds(pl.multiple_of(g * BLOCK_TOKENS, BLOCK_TOKENS), BLOCK_TOKENS)
            dq_s[at, :] = dq.astype(dq_s.dtype)
            for n, b in enumerate(ids):
                at = pl.ds(pl.multiple_of(b * BLOCK_TOKENS, BLOCK_TOKENS), BLOCK_TOKENS)
                part = slice(n * BLOCK_TOKENS, (n + 1) * BLOCK_TOKENS)
                dk_s[at, :] += dk[part]
                dv_s[at, :] += dv[part]
        return carry

    lax.fori_loop(0, count // unroll, body, 0)
    rows = out_ref.shape[1] // 3

    def store(c, carry):
        at = pl.ds(pl.multiple_of(c * rows, rows), rows)
        for j, ref in enumerate((dq_s, dk_s, dv_s)):
            out_ref[c, j * rows : (j + 1) * rows, :] = ref[at, :].astype(out_ref.dtype)
        return carry

    lax.fori_loop(0, out_ref.shape[0], store, 0)


def unroll_for(count, most):
    return max(u for u in range(1, most + 1) if count % u == 0)


def params():
    return pltpu.CompilerParams(vmem_limit_bytes=VMEM_LIMIT)


def per_device(queries, key_rows, values, rand_blocks, out_weight, cotangent):
    bf16, f32 = jnp.bfloat16, jnp.float32
    dp_count = lax.axis_size("dp")
    hi_count = lax.axis_size("hi")
    lo_count = lax.axis_size("lo")
    head_count = lax.axis_size("head")
    seq_count = hi_count * lo_count
    group = lo_count * head_count
    rows, width = queries.shape[1], queries.shape[2]
    range_rows = rows * head_count
    own_rows = rows * group
    rand_count = rand_blocks.shape[2]
    head_dim = HEAD_SIZE

    packed = pl.pallas_call(
        functools.partial(pack_kernel, lo_count, head_count),
        out_shape=jax.ShapeDtypeStruct((group, 3 * rows, head_dim), bf16),
        in_specs=[vmem()] * 3,
        out_specs=vmem(),
        compiler_params=params(),
        name="pack_heads",
    )(queries[0], key_rows[0], values[0])
    packed = lax.all_to_all(packed, ("lo", "head"), split_axis=0, concat_axis=0, tiled=True)
    if hi_count > 1:
        packed = lax.all_gather(packed, "hi", axis=0, tiled=True)
    ids = lax.all_to_all(
        jnp.transpose(rand_blocks, (1, 0, 2)), "lo", split_axis=0, concat_axis=0, tiled=True
    ).reshape(-1)
    block_count = own_rows // BLOCK_TOKENS
    offset = (lax.axis_index("hi") * block_count).astype(jnp.int32).reshape(1)
    all_rows = own_rows * hi_count
    held = pltpu.VMEM((all_rows, head_dim), bf16)
    summed = pltpu.VMEM((all_rows, head_dim), f32)
    pair = 2 * own_rows * 8 * BLOCK_TOKENS * head_dim

    cot_rows = lax.all_gather(cotangent[0], "head", axis=0, tiled=True)
    weight_heads = out_weight.reshape(lo_count, head_dim, width)
    grad_piece = jnp.einsum(
        "te,hde->htd", cot_rows, weight_heads, preferred_element_type=f32
    ).astype(bf16)
    grad_rows = lax.all_to_all(
        grad_piece, "lo", split_axis=0, concat_axis=0, tiled=True
    ).reshape(own_rows, head_dim)

    attn = pl.pallas_call(
        functools.partial(forward_kernel, rand_count, unroll_for(block_count, 4)),
        out_shape=jax.ShapeDtypeStruct((own_rows, head_dim), bf16),
        in_specs=[smem(), smem(), vmem()],
        out_specs=vmem(),
        scratch_shapes=[held] * 3,
        compiler_params=params(),
        cost_estimate=pl.CostEstimate(
            flops=8 * pair, bytes_accessed=4 * own_rows * head_dim * 2,
            transcendentals=own_rows * 8 * BLOCK_TOKENS,
        ),
        name="attention_forward",
    )(offset, ids, packed)

    attn_heads = lax.all_to_all(
        attn.reshape(lo_count, range_rows, head_dim), "lo", split_axis=0, concat_axis=0, tiled=True
    )
    weight_acc = jnp.einsum(
        "htd,te->hde", attn_heads, cot_rows, preferred_element_type=f32
    ).reshape(lo_count * head_dim, width)

    grads = pl.pallas_call(
        functools.partial(backward_kernel, rand_count, unroll_for(block_count, 2)),
        out_shape=jax.ShapeDtypeStruct(
            (group * hi_count, 3 * rows, head_dim), bf16 if hi_count == 1 else f32
        ),
        in_specs=[smem(), smem(), vmem(), vmem(), vmem()],
        out_specs=vmem(),
        scratch_shapes=[held] * 3 + [pltpu.VMEM((all_rows, head_dim), f32), summed, summed],
        compiler_params=params(),
        cost_estimate=pl.CostEstimate(
            flops=20 * pair, bytes_accessed=8 * own_rows * head_dim * 2,
            transcendentals=own_rows * 8 * BLOCK_TOKENS,
        ),
        name="attention_backward",
    )(offset, ids, packed, attn, grad_rows)

    half = weight_acc.shape[0] // dp_count
    dp_index = lax.axis_index("dp")
    own_half = lax.dynamic_slice_in_dim(weight_acc, dp_index * half, half, axis=0)
    other_half = lax.dynamic_slice_in_dim(weight_acc, (1 - dp_index) * half, half, axis=0)
    swapped = lax.ppermute(other_half.astype(bf16), "dp", [(0, 1), (1, 0)])
    half_sum = own_half + swapped.astype(f32)
    pieces = lax.all_to_all(
        half_sum.astype(bf16), ("hi", "lo"), split_axis=0, concat_axis=0, tiled=True
    ).reshape(seq_count, half // seq_count, width)
    token_total = dp_count * seq_count * range_rows
    piece = jnp.sum(pieces.astype(f32), axis=0) * (1.0 / math.sqrt(token_total))
    weight_grad = lax.all_gather(
        piece.astype(bf16), ("dp", "hi", "lo"), axis=0, tiled=True
    ).astype(f32)

    partial = jnp.einsum(
        "htd,hde->te", attn_heads, weight_heads, preferred_element_type=f32
    ).astype(bf16)
    parts = lax.all_to_all(partial, "head", split_axis=0, concat_axis=0, tiled=True)
    layer_out = jnp.sum(
        parts.reshape(head_count, rows, width).astype(f32), axis=0
    ).astype(bf16)

    if hi_count > 1:
        grads = lax.psum_scatter(grads, "hi", scatter_dimension=0, tiled=True).astype(bf16)
    returned = lax.all_to_all(grads, ("lo", "head"), split_axis=0, concat_axis=0, tiled=True)
    grad_q, grad_k, grad_v = pl.pallas_call(
        functools.partial(unpack_kernel, lo_count, head_count),
        out_shape=[jax.ShapeDtypeStruct((rows, width), bf16)] * 3,
        in_specs=[vmem()],
        out_specs=[vmem()] * 3,
        compiler_params=params(),
        name="unpack_heads",
    )(returned)
    return (layer_out[None], grad_q[None], grad_k[None], grad_v[None], weight_grad)


def solution(mesh):
    dp, seq, head = (mesh.shape[name] for name in ("dp", "seq", "head"))
    heads = 16
    lo = heads // head
    cut = Mesh(mesh.devices.reshape(dp, seq // lo, lo, head), ("dp", "hi", "lo", "head"))
    tokens = P("dp", ("hi", "lo", "head"), None)
    return jax.shard_map(
        per_device,
        mesh=cut,
        in_specs=(tokens, tokens, tokens, P(("hi", "lo"), "head", None), P("head", None), tokens),
        out_specs=(tokens, tokens, tokens, tokens, P("head", None)),
        check_vma=False,
    )
```

time: 914 us -> 282 us (0.31); the launches traced: 901 us -> 280 us
  local copies, waits for them, and re-layouts: 323 us -> 12.5 us
  other arithmetic: 173 us -> 11.5 us
  waiting for transfers between devices: 290 us -> 148 us
  Pallas kernels: 0 us -> 41.7 us
  matrix products: 39.3 us -> 10.5 us
  starting transfers between devices: 59.8 us -> 42.1 us
    psum x3 -> x0, waiting for transfers between devices: 209 us -> none  [the longest x1 110 us: per_device(): global_grad = lax.psum(jnp.stack([key_first, value_first], axis=1), 'seq')]
    all_to_all x9 -> x7, waiting for transfers between devices: 23.8 us -> 147 us  [the longest x1 56.8 us: per_device(): lax.all_to_all(grads, ('lo', 'head'), split_axis=0, concat_axis=0, tiled=...]
    scatter-add x6 -> x0, other arithmetic: 62.6 us -> none  [the longest x1 50.9 us: per_device(): core = core.at[asked_block, :, :, asked_head, :].add(incoming)]
    ppermute x4 -> x1, waiting for transfers between devices: 56.9 us -> 0.01 us  [per_device(): swapped = lax.ppermute(other_half.astype(bf16), 'dp', [(0, 1), (1, 0)])]
    unnamed x7 -> x0, other arithmetic: 55.6 us -> none
    gather x4 -> x0, local copies, waits for them, and re-layouts: 52.1 us -> none  [the longest x3 40.9 us: per_device(): served = block_view[asked_block, :, :, asked_head, :]]
    reshape x11 -> x1, local copies, waits for them, and re-layouts: 51.7 us -> 0.1 us  [per_device(): ids = lax.all_to_all(jnp.transpose(rand_blocks, (1, 0, 2)), 'lo', split_a...]
    unnamed x64 -> x24, local copies, waits for them, and re-layouts: 58.8 us -> 9.68 us
  transfers between devices with their start and end apart: 18 -> 10, of which waited for: 8 -> 6; matrix products, arithmetic and copies ran while one was open for 49% -> 6% of each run, Pallas kernels for 0% -> 15%
where the time goes in v1:
time: 282 us; the launch traced here: 280 us
  waiting for transfers between devices  148 us (52%)
  starting transfers between devices  42.1 us (15%)
  Pallas kernels  41.7 us (15%)
  between operations  14.2 us (5%)
  local copies, waits for them, and re-layouts  12.5 us (4%)
  other arithmetic  11.5 us (4%)
  matrix products  10.5 us (4%)
    all_to_all x1, waiting for transfers between devices, per_device(): lax.all_to_all(grads, ('lo', 'head'), split_axis=0, concat_axis=0, tiled=...  56.8 us
    all_to_all x1, waiting for transfers between devices, per_device(): lax.all_to_all(packed, ('lo', 'head'), split_axis=0, concat_axis=0, tiled...  43.5 us
    pallas_call x1, Pallas kernels, per_device(): pl.pallas_call(functools.partial(backward_kernel, rand_count, unroll_for(...  23.9 us
    all_to_all x1, waiting for transfers between devices, per_device(): lax.all_to_all(half_sum.astype(bf16), ('hi', 'lo'), split_axis=0, concat_...  18.8 us
    pallas_call x1, Pallas kernels, per_device(): pl.pallas_call(functools.partial(forward_kernel, rand_count, unroll_for(b...  14.1 us
    all_to_all x1, waiting for transfers between devices, per_device(): lax.all_to_all(attn.reshape(lo_count, range_rows, head_dim), 'lo', split_...  12.4 us
    all_to_all x1, waiting for transfers between devices, per_device(): lax.all_to_all(grad_piece, 'lo', split_axis=0, concat_axis=0, tiled=True)  11.8 us
    unnamed x24, local copies, waits for them, and re-layouts  9.68 us
  transfers between devices with their start and end apart: 10, of which 6 were waited for; matrix products, arithmetic and copies ran while one was open for 6% of the time, Pallas kernels for 15%

profile of v1, /device:TPU:16, one launch (start us, length us, event | category | flops | bytes accessed | tf_op | source)
XLA Modules:
  0.0 280.0 jit_solution(16013715519259288803)
XLA Ops:
  7.2 0.0 copy-start
  7.2 5.3 %all-to-all-start = ((s32[4,10,4]{1,2,0:T(4,128)}), s32[4,10,4]{1,2,0:T(4,128)S(1)}, u32[]{:S(2)}, u32[]{:S(2)}) async-start(s32[4,10,4]{1,2,0:T(4,128)} %bitcast.42), calls=%async_computation | async-start | bytes 16384 | tf_op jit(solution)/shard_map/all_to_all | solution.py:206
  12.5 0.0 copy-start.3
  12.5 1.1 copy-done.3
  13.6 0.0 copy-start.4
  13.6 1.1 copy-done.4
  14.7 0.0 copy-start.5
  14.7 1.1 copy-done.5
  15.8 0.3 pack_heads.1
  16.1 0.0 copy-start.1
  16.2 1.3 copy-done.1
  17.4 0.0 all-to-all-done
  17.4 7.0 %all-to-all-start.1 = ((bf16[16,480,128]{2,1,0:T(8,128)(2,1)}), bf16[16,480,128]{2,1,0:T(8,128)(2,1)}, u32[]{:S(2)}, u32[]{:S(2)}) async-start(bf16[16,480,128]{2,1,0:T(8,128)(2,1)} %copy-done.1), calls=%async_computation.1 | async-start | bytes 3932160 | tf_op jit(solution)/shard_map/all_to_all | solution.py:203
  24.4 0.0 all-gather.6.cloned.1.call-start
  24.5 0.7 all-gather.6.cloned.1.call-update
  25.2 0.1 copy.13
  25.3 0.1 reshape.34.idx_ref
  25.4 43.5 %all-to-all-done.1.packed_ref = bf16[16,480,128]{2,1,0:T(8,128)(2,1)} async-done(((bf16[16,480,128]{2,1,0:T(8,128)(2,1)}), bf16[16,480,128]{2,1,0:T(8,128)(2,1)}, u32[]{:S(2)}, u32[]{:S(2)}) %all-to-all-start.1) | async-done | bytes 1966112 | tf_op jit(solution)/shard_map/all_to_all | solution.py:203
  68.9 14.1 %attention_forward.1.attn_ref = bf16[2560,128]{1,0:T(8,128)(2,1)} custom-call(s32[1]{0:T(128)} %constant.7.clone.1.off_ref, s32[160]{0:T(256)S(1)} %reshape.34.idx_ref, bf16[16,480,128]{2,1,0:T(8,128)(2,1)} %all-to-all-done.1.packed_ref), custom_call_target="tpu_custom_call" | custom-call | flops 2684354560 | bytes 2621440 | tf_op jit(solution)/shard_map/attention_forward/pallas_call | solution.py:225
  82.9 4.2 %all-to-all-start.2 = ((bf16[4,640,128]{2,1,0:T(8,128)(2,1)}), bf16[4,640,128]{2,1,0:T(8,128)(2,1)S(1)}, u32[]{:S(2)}, u32[]{:S(2)}) async-start(bf16[4,640,128]{2,1,0:T(8,128)(2,1)} %bitcast.4), calls=%async_computation.2 | async-start | bytes 1310720 | tf_op jit(solution)/shard_map/all_to_all | solution.py:239
  87.1 0.0 all-gather.6.cloned.1.call-done
  87.1 12.4 %all-to-all-done.2 = bf16[4,640,128]{2,1,0:T(8,128)(2,1)S(1)} async-done(((bf16[4,640,128]{2,1,0:T(8,128)(2,1)}), bf16[4,640,128]{2,1,0:T(8,128)(2,1)S(1)}, u32[]{:S(2)}, u32[]{:S(2)}) %all-to-all-start.2) | async-done | bytes 655392 | tf_op jit(solution)/shard_map/all_to_all | solution.py:239
  99.6 0.0 copy-start.9
  99.6 0.0 copy-start.10
  99.6 3.9 %fusion = f32[4,128,2048]{2,1,0:T(8,128)S(1)} fusion(bf16[4,640,128]{2,1,0:T(8,128)(2,1)S(1)} %all-to-all-done.2, bf16[1,640,2048]{2,1,0:T(8,128)(2,1)} %all-gather.6.cloned.1.call-done), kind=kOutput, calls=%fused_computation.1 | convolution fusion | flops 1342177280 | bytes 7471104 | tf_op jit(solution)/shard_map/htd,te->hde/dot_general | solution.py:242
  103.5 0.0 copy-done.9
  103.5 0.0 copy-start.6
  103.5 2.0 copy-done.6
  105.5 1.1 dynamic-slice_convert_fusion
  106.6 0.0 collective-permute-start
  106.6 0.0 copy-done
  106.6 0.0 copy-done.10
  106.6 2.8 fusion.7
  109.4 6.7 %all-to-all-start.4 = ((bf16[4,640,128]{1,2,0:T(8,128)(2,1)}), bf16[4,640,128]{1,2,0:T(8,128)(2,1)S(1)}, u32[]{:S(2)}, u32[]{:S(2)}) async-start(bf16[4,640,128]{1,2,0:T(8,128)(2,1)} %fusion.7), calls=%async_computation.4 | async-start | bytes 1310720 | tf_op jit(solution)/shard_map/all_to_all | solution.py:221
  116.1 0.0 collective-permute-done
  116.1 3.2 %add_convert_fusion = bf16[256,2048]{1,0:T(8,128)(2,1)} fusion(bf16[256,2048]{1,0:T(8,128)(2,1)} %collective-permute-done, f32[512,2048]{1,0:T(8,128)} %bitcast.39, s32[]{:T(128)S(6)} %select_n.6), kind=kLoop, calls=%fused_computation.6 | loop fusion | flops 1572864 | bytes 4194308 | tf_op jit(solution)/shard_map/convert_element_type | solution.py:269
  119.3 11.8 %all-to-all-done.4 = bf16[4,640,128]{1,2,0:T(8,128)(2,1)S(1)} async-done(((bf16[4,640,128]{1,2,0:T(8,128)(2,1)}), bf16[4,640,128]{1,2,0:T(8,128)(2,1)S(1)}, u32[]{:S(2)}, u32[]{:S(2)}) %all-to-all-start.4) | async-done | bytes 655392 | tf_op jit(solution)/shard_map/all_to_all | solution.py:221
  131.1 0.0 copy-start.11
  131.1 0.8 copy-done.11
  131.9 6.8 %all-to-all-start.6 = ((bf16[4,64,2048]{2,1,0:T(8,128)(2,1)}), bf16[4,64,2048]{2,1,0:T(8,128)(2,1)S(1)}, u32[]{:S(2)}, u32[]{:S(2)}) async-start(bf16[4,64,2048]{2,1,0:T(8,128)(2,1)} %bitcast.17), calls=%async_computation.6 | async-start | bytes 2097152 | tf_op jit(solution)/shard_map/all_to_all | solution.py:268
  138.7 3.9 %bitcast_convert_fusion = bf16[640,2048]{1,0:T(8,128)(2,1)} fusion(bf16[4,640,128]{2,1,0:T(8,128)(2,1)} %copy-done.9, bf16[4,128,2048]{2,1,0:T(8,128)(2,1)S(1)} %bitcast.32), kind=kOutput, calls=%fused_computation | convolution fusion | flops 1343488000 | bytes 5373952 | tf_op jit(solution)/shard_map/htd,hde->te/dot_general | solution.py:277
  142.5 18.8 %all-to-all-done.6 = bf16[4,64,2048]{2,1,0:T(8,128)(2,1)S(1)} async-done(((bf16[4,64,2048]{2,1,0:T(8,128)(2,1)}), bf16[4,64,2048]{2,1,0:T(8,128)(2,1)S(1)}, u32[]{:S(2)}, u32[]{:S(2)}) %all-to-all-start.6) | async-done | bytes 1048608 | tf_op jit(solution)/shard_map/all_to_all | solution.py:268
  161.3 0.0 copy-start.7
  161.3 1.0 copy-done.7
  162.3 4.6 %all-to-all-start.3 = ((bf16[4,160,2048]{2,1,0:T(8,128)(2,1)}), bf16[4,160,2048]{2,1,0:T(8,128)(2,1)}, u32[]{:S(2)}, u32[]{:S(2)}) async-start(bf16[4,160,2048]{2,1,0:T(8,128)(2,1)} %bitcast.40), calls=%async_computation.3 | async-start | bytes 5242880 | tf_op jit(solution)/shard_map/all_to_all | solution.py:280
  166.8 1.4 copy.14
  168.3 0.0 copy-start.8
  168.3 23.9 %attention_backward.1 = bf16[16,480,128]{2,1,0:T(8,128)(2,1)S(1)} custom-call(s32[1]{0:T(128)} %constant.7.clone.1.off_ref, s32[160]{0:T(256)S(1)} %reshape.34.idx_ref, bf16[16,480,128]{2,1,0:T(8,128)(2,1)} %all-to-all-done.1.packed_ref, bf16[2560,128]{1,0:T(8,128)(2,1)} %attention_forward.1.attn_ref, bf16[2560,128]{1,0:T(8,128)(2,1)S(1)} %bitcast.34), custom_call_target="tpu_custom_call" | custom-call | flops 6710886400 | bytes 5242880 | tf_op jit(solution)/shard_map/attention_backward/pallas_call | solution.py:246
  192.2 0.0 copy-start.2
  192.2 1.3 copy-done.2
  193.5 0.0 copy-done.8
  193.5 0.2 convert_reduce_fusion
  193.7 3.6 %all-to-all-done.3 = bf16[4,160,2048]{2,1,0:T(8,128)(2,1)} async-done(((bf16[4,160,2048]{2,1,0:T(8,128)(2,1)}), bf16[4,160,2048]{2,1,0:T(8,128)(2,1)}, u32[]{:S(2)}, u32[]{:S(2)}) %all-to-all-start.3) | async-done | bytes 2621472 | tf_op jit(solution)/shard_map/all_to_all | solution.py:280
  197.3 7.5 %all-to-all-start.5 = ((bf16[16,480,128]{2,1,0:T(8,128)(2,1)}), bf16[16,480,128]{2,1,0:T(8,128)(2,1)}, u32[]{:S(2)}, u32[]{:S(2)}) async-start(bf16[16,480,128]{2,1,0:T(8,128)(2,1)} %copy-done.2), calls=%async_computation.5 | async-start | bytes 3932160 | tf_op jit(solution)/shard_map/all_to_all | solution.py:287
  204.8 0.0 all-gather.4.cloned.1.call-start
  204.9 0.7 multiply_convert_fusion
  205.6 0.0 all-gather.4.cloned.1.call-update
  205.6 3.3 %reduce_sum.21 = bf16[160,2048]{1,0:T(8,128)(2,1)} reduce(bf16[4,160,2048]{2,1,0:T(8,128)(2,1)} %all-to-all-done.3, bf16[]{:T(256)} %constant.8.clone.1), dimensions={0}, to_apply=%region_0.0 | reduce | flops 983040 | bytes 3276802 | tf_op jit(solution)/shard_map/reduce_sum | solution.py:281
  208.9 56.8 %all-to-all-done.5.in_ref = bf16[16,480,128]{2,1,0:T(8,128)(2,1)} async-done(((bf16[16,480,128]{2,1,0:T(8,128)(2,1)}), bf16[16,480,128]{2,1,0:T(8,128)(2,1)}, u32[]{:S(2)}, u32[]{:S(2)}) %all-to-all-start.5) | async-done | bytes 1966112 | tf_op jit(solution)/shard_map/all_to_all | solution.py:287
  265.6 3.4 %unpack_heads.1 = (bf16[160,2048]{1,0:T(8,128)(2,1)}, bf16[160,2048]{1,0:T(8,128)(2,1)}, bf16[160,2048]{1,0:T(8,128)(2,1)}) custom-call(bf16[16,480,128]{2,1,0:T(8,128)(2,1)} %all-to-all-done.5.in_ref), custom_call_target="tpu_custom_call" | custom-call | tf_op jit(solution)/shard_map/unpack_heads/pallas_call | solution.py:288
  269.0 0.0 all-gather.4.cloned.1.call-done
  269.0 4.1 %convert_element_type.37 = f32[512,2048]{1,0:T(8,128)} convert(bf16[512,2048]{1,0:T(8,128)(2,1)} %all-gather.4.cloned.1.call-done) | non-fusion elementwise | flops 1048576 | bytes 6291456 | tf_op jit(solution)/shard_map/convert_element_type | solution.py:275
Async XLA Ops:
  7.2 99.5 %copy-start = (bf16[512,2048]{1,0:T(8,128)(2,1)S(1)}, bf16[512,2048]{1,0:T(8,128)(2,1)}, u32[]{:S(2)}) copy-start(bf16[512,2048]{1,0:T(8,128)(2,1)} %param.10) | copy-start | bytes 6291460
  7.2 10.2 %all-to-all-start = ((s32[4,10,4]{1,2,0:T(4,128)}), s32[4,10,4]{1,2,0:T(4,128)S(1)}, u32[]{:S(2)}, u32[]{:S(2)}) async-start(s32[4,10,4]{1,2,0:T(4,128)} %bitcast.42), calls=%async_computation | async-start | bytes 16384 | tf_op jit(solution)/shard_map/all_to_all | solution.py:206
  12.5 1.1 copy-start.3
  13.6 1.1 copy-start.4
  14.7 1.1 copy-start.5
  16.1 1.3 copy-start.1
  17.4 51.4 %all-to-all-start.1 = ((bf16[16,480,128]{2,1,0:T(8,128)(2,1)}), bf16[16,480,128]{2,1,0:T(8,128)(2,1)}, u32[]{:S(2)}, u32[]{:S(2)}) async-start(bf16[16,480,128]{2,1,0:T(8,128)(2,1)} %copy-done.1), calls=%async_computation.1 | async-start | bytes 3932160 | tf_op jit(solution)/shard_map/all_to_all | solution.py:203
  24.4 62.7 %all-gather.6.cloned.1.call-start = ((), (), s32[]{:S(2)}) async-start(), calls=%async_computation.8 | async-start | bytes 3276800 | tf_op jit(solution)/shard_map/all_gather | solution.py:216
  82.9 16.6 %all-to-all-start.2 = ((bf16[4,640,128]{2,1,0:T(8,128)(2,1)}), bf16[4,640,128]{2,1,0:T(8,128)(2,1)S(1)}, u32[]{:S(2)}, u32[]{:S(2)}) async-start(bf16[4,640,128]{2,1,0:T(8,128)(2,1)} %bitcast.4), calls=%async_computation.2 | async-start | bytes 1310720 | tf_op jit(solution)/shard_map/all_to_all | solution.py:239
  99.6 3.9 %copy-start.9 = (bf16[4,640,128]{2,1,0:T(8,128)(2,1)}, bf16[4,640,128]{2,1,0:T(8,128)(2,1)S(1)}, u32[]{:S(2)}) copy-start(bf16[4,640,128]{2,1,0:T(8,128)(2,1)S(1)} %all-to-all-done.2) | copy-start | bytes 1966084
  99.6 7.1 %copy-start.10 = (bf16[1,640,2048]{2,1,0:T(8,128)(2,1)S(1)}, bf16[1,640,2048]{2,1,0:T(8,128)(2,1)}, u32[]{:S(2)}) copy-start(bf16[1,640,2048]{2,1,0:T(8,128)(2,1)} %all-gather.6.cloned.1.call-done) | copy-start | bytes 7864324
  103.5 2.0 copy-start.6
  106.6 9.5 %collective-permute-start = (bf16[256,2048]{1,0:T(8,128)(2,1)}, bf16[256,2048]{1,0:T(8,128)(2,1)}, u32[]{:S(2)}, u32[]{:S(2)}) collective-permute-start(bf16[256,2048]{1,0:T(8,128)(2,1)} %dynamic-slice_convert_fusion), channel_id=1, source_target_pairs={{0,16},{16,0},{1,17},{17,1},{2,18},{18,2},{3,19},{19,3},{4,20},{20... | collective-permute-start | bytes 3145736 | tf_op jit(solution)/shard_map/ppermute | solution.py:266
  109.4 21.7 %all-to-all-start.4 = ((bf16[4,640,128]{1,2,0:T(8,128)(2,1)}), bf16[4,640,128]{1,2,0:T(8,128)(2,1)S(1)}, u32[]{:S(2)}, u32[]{:S(2)}) async-start(bf16[4,640,128]{1,2,0:T(8,128)(2,1)} %fusion.7), calls=%async_computation.4 | async-start | bytes 1310720 | tf_op jit(solution)/shard_map/all_to_all | solution.py:221
  131.1 0.8 copy-start.11
  131.9 29.4 %all-to-all-start.6 = ((bf16[4,64,2048]{2,1,0:T(8,128)(2,1)}), bf16[4,64,2048]{2,1,0:T(8,128)(2,1)S(1)}, u32[]{:S(2)}, u32[]{:S(2)}) async-start(bf16[4,64,2048]{2,1,0:T(8,128)(2,1)} %bitcast.17), calls=%async_computation.6 | async-start | bytes 2097152 | tf_op jit(solution)/shard_map/all_to_all | solution.py:268
  161.3 1.0 copy-start.7
  162.3 35.0 %all-to-all-start.3 = ((bf16[4,160,2048]{2,1,0:T(8,128)(2,1)}), bf16[4,160,2048]{2,1,0:T(8,128)(2,1)}, u32[]{:S(2)}, u32[]{:S(2)}) async-start(bf16[4,160,2048]{2,1,0:T(8,128)(2,1)} %bitcast.40), calls=%async_computation.3 | async-start | bytes 5242880 | tf_op jit(solution)/shard_map/all_to_all | solution.py:280
  168.3 25.3 %copy-start.8 = (bf16[4,64,2048]{2,1,0:T(8,128)(2,1)S(1)}, bf16[4,64,2048]{2,1,0:T(8,128)(2,1)}, u32[]{:S(2)}) copy-start(bf16[4,64,2048]{2,1,0:T(8,128)(2,1)} %copy-done.7) | copy-start | bytes 3145732
  192.2 1.3 copy-start.2
  197.3 68.3 %all-to-all-start.5 = ((bf16[16,480,128]{2,1,0:T(8,128)(2,1)}), bf16[16,480,128]{2,1,0:T(8,128)(2,1)}, u32[]{:S(2)}, u32[]{:S(2)}) async-start(bf16[16,480,128]{2,1,0:T(8,128)(2,1)} %copy-done.2), calls=%async_computation.5 | async-start | bytes 3932160 | tf_op jit(solution)/shard_map/all_to_all | solution.py:287
  204.8 64.2 %all-gather.4.cloned.1.call-start = ((), (), s32[]{:S(2)}) async-start(), calls=%async_computation.7 | async-start | bytes 2359296 | tf_op jit(solution)/shard_map/all_gather | solution.py:273
Sparse Core Ops, SparseCore 0:
  27.1 55.4 all-gather.5
  207.8 46.4 all-gather.3

commit v2 on v1

--- a/solution.py
+++ b/solution.py
@@ -74,10 +74,14 @@
     return ref[pl.ds(pl.multiple_of(b * BLOCK_TOKENS, BLOCK_TOKENS), BLOCK_TOKENS), :]
 
 
-def slots_of(i, off_ref, idx_ref, rand_count, total):
+def slots_of(i, off_ref, idx_ref, dims, total):
+    lo_count, blocks, rand_count = dims
     g = off_ref[0] + i
+    me = off_ref[1]
+    piece = (i // blocks) ^ me
+    base = ((piece * blocks + i % blocks) * lo_count + me) * rand_count
     ids = [jnp.maximum(g - 1, 0), g, jnp.minimum(g + 1, total - 1), jnp.int32(0)]
-    ids += [idx_ref[i * rand_count + r] for r in range(rand_count)]
+    ids += [idx_ref[base + r] for r in range(rand_count)]
     return g, ids
 
 
@@ -89,7 +93,7 @@
 
 
 def forward_kernel(
-    rand_count, unroll, off_ref, idx_ref, packed_ref, attn_ref, q_s, k_s, v_s
+    dims, unroll, off_ref, idx_ref, packed_ref, attn_ref, q_s, k_s, v_s
 ):
     total = k_s.shape[0] // BLOCK_TOKENS
     load_chunks(packed_ref, (q_s, k_s, v_s))
@@ -99,7 +103,7 @@
         results = []
         for u in range(unroll):
             i = step * unroll + u
-            g, ids = slots_of(i, off_ref, idx_ref, rand_count, total)
+            g, ids = slots_of(i, off_ref, idx_ref, dims, total)
             keys = jnp.concatenate([block_at(k_s, b) for b in ids], axis=0)
             vals = jnp.concatenate([block_at(v_s, b) for b in ids], axis=0)
             s = masked_scores(block_at(q_s, g), keys, g, total)
@@ -115,7 +119,7 @@
 
 
 def backward_kernel(
-    rand_count, unroll, off_ref, idx_ref, packed_ref, attn_ref, grad_ref, out_ref,
+    dims, unroll, off_ref, idx_ref, packed_ref, attn_ref, grad_ref, out_ref,
     q_s, k_s, v_s, dq_s, dk_s, dv_s,
 ):
     total = k_s.shape[0] // BLOCK_TOKENS
@@ -130,7 +134,7 @@
         results = []
         for u in range(unroll):
             i = step * unroll + u
-            g, ids = slots_of(i, off_ref, idx_ref, rand_count, total)
+            g, ids = slots_of(i, off_ref, idx_ref, dims, total)
             keys = jnp.concatenate([block_at(k_s, b) for b in ids], axis=0)
             vals = jnp.concatenate([block_at(v_s, b) for b in ids], axis=0)
             q = block_at(q_s, g)
@@ -174,6 +178,41 @@
     return max(u for u in range(1, most + 1) if count % u == 0)
 
 
+def swap_pieces(send, axis):
+    count = lax.axis_size(axis)
+    return [
+        lax.ppermute(send(k), axis, [(i, i ^ k) for i in range(count)]) for k in range(1, count)
+    ]
+
+
+def chunk_for(x, index):
+    return lax.dynamic_slice_in_dim(x, index, 1, axis=0)[0]
+
+
+def scatter_sum(x, axis):
+    count = lax.axis_size(axis)
+    me = lax.axis_index(axis)
+    x = x.reshape((count, x.shape[0] // count) + x.shape[1:])
+    if count > 4:
+        pieces = lax.all_to_all(
+            x.astype(jnp.bfloat16), axis, split_axis=0, concat_axis=0, tiled=True
+        )
+        return jnp.sum(pieces.astype(jnp.float32), axis=0)
+    total = chunk_for(x, me).astype(jnp.float32)
+    for piece in swap_pieces(lambda k: chunk_for(x, me ^ k).astype(jnp.bfloat16), axis):
+        total = total + piece.astype(jnp.float32)
+    return total
+
+
+def gather_rows(x, axis):
+    rows = x.shape[0]
+    me = lax.axis_index(axis)
+    whole = jnp.zeros((rows * lax.axis_size(axis),) + x.shape[1:], x.dtype)
+    for k, piece in enumerate([x] + swap_pieces(lambda k: x, axis)):
+        whole = lax.dynamic_update_slice_in_dim(whole, piece, (me ^ k) * rows, axis=0)
+    return whole
+
+
 def params():
     return pltpu.CompilerParams(vmem_limit_bytes=VMEM_LIMIT)
 
@@ -203,27 +242,28 @@
     packed = lax.all_to_all(packed, ("lo", "head"), split_axis=0, concat_axis=0, tiled=True)
     if hi_count > 1:
         packed = lax.all_gather(packed, "hi", axis=0, tiled=True)
-    ids = lax.all_to_all(
-        jnp.transpose(rand_blocks, (1, 0, 2)), "lo", split_axis=0, concat_axis=0, tiled=True
-    ).reshape(-1)
+    id_pieces = [rand_blocks] + swap_pieces(lambda k: rand_blocks, "lo")
+    ids = jnp.stack(id_pieces).reshape(-1)
+    dims = (lo_count, rand_blocks.shape[0], rand_count)
     block_count = own_rows // BLOCK_TOKENS
-    offset = (lax.axis_index("hi") * block_count).astype(jnp.int32).reshape(1)
+    offset = jnp.stack([lax.axis_index("hi") * block_count, lax.axis_index("lo")]).astype(jnp.int32)
     all_rows = own_rows * hi_count
     held = pltpu.VMEM((all_rows, head_dim), bf16)
     summed = pltpu.VMEM((all_rows, head_dim), f32)
     pair = 2 * own_rows * 8 * BLOCK_TOKENS * head_dim
 
-    cot_rows = lax.all_gather(cotangent[0], "head", axis=0, tiled=True)
+    cot_rows = gather_rows(cotangent[0], "head")
     weight_heads = out_weight.reshape(lo_count, head_dim, width)
     grad_piece = jnp.einsum(
         "te,hde->htd", cot_rows, weight_heads, preferred_element_type=f32
     ).astype(bf16)
+    packed, grad_piece = lax.optimization_barrier((packed, grad_piece))
     grad_rows = lax.all_to_all(
         grad_piece, "lo", split_axis=0, concat_axis=0, tiled=True
     ).reshape(own_rows, head_dim)
 
     attn = pl.pallas_call(
-        functools.partial(forward_kernel, rand_count, unroll_for(block_count, 4)),
+        functools.partial(forward_kernel, dims, unroll_for(block_count, 4)),
         out_shape=jax.ShapeDtypeStruct((own_rows, head_dim), bf16),
         in_specs=[smem(), smem(), vmem()],
         out_specs=vmem(),
@@ -239,12 +279,8 @@
     attn_heads = lax.all_to_all(
         attn.reshape(lo_count, range_rows, head_dim), "lo", split_axis=0, concat_axis=0, tiled=True
     )
-    weight_acc = jnp.einsum(
-        "htd,te->hde", attn_heads, cot_rows, preferred_element_type=f32
-    ).reshape(lo_count * head_dim, width)
-
     grads = pl.pallas_call(
-        functools.partial(backward_kernel, rand_count, unroll_for(block_count, 2)),
+        functools.partial(backward_kernel, dims, unroll_for(block_count, 4)),
         out_shape=jax.ShapeDtypeStruct(
             (group * hi_count, 3 * rows, head_dim), bf16 if hi_count == 1 else f32
         ),
@@ -259,28 +295,26 @@
         name="attention_backward",
     )(offset, ids, packed, attn, grad_rows)
 
+    attn_heads, grads = lax.optimization_barrier((attn_heads, grads))
+    weight_acc = jnp.einsum(
+        "htd,te->hde", attn_heads, cot_rows, preferred_element_type=f32
+    ).reshape(lo_count * head_dim, width)
+
     half = weight_acc.shape[0] // dp_count
     dp_index = lax.axis_index("dp")
     own_half = lax.dynamic_slice_in_dim(weight_acc, dp_index * half, half, axis=0)
     other_half = lax.dynamic_slice_in_dim(weight_acc, (1 - dp_index) * half, half, axis=0)
     swapped = lax.ppermute(other_half.astype(bf16), "dp", [(0, 1), (1, 0)])
     half_sum = own_half + swapped.astype(f32)
-    pieces = lax.all_to_all(
-        half_sum.astype(bf16), ("hi", "lo"), split_axis=0, concat_axis=0, tiled=True
-    ).reshape(seq_count, half // seq_count, width)
     token_total = dp_count * seq_count * range_rows
-    piece = jnp.sum(pieces.astype(f32), axis=0) * (1.0 / math.sqrt(token_total))
+    ranges = "lo" if hi_count == 1 else ("hi", "lo")
+    piece = scatter_sum(half_sum, ranges) * (1.0 / math.sqrt(token_total))
     weight_grad = lax.all_gather(
         piece.astype(bf16), ("dp", "hi", "lo"), axis=0, tiled=True
     ).astype(f32)
 
-    partial = jnp.einsum(
-        "htd,hde->te", attn_heads, weight_heads, preferred_element_type=f32
-    ).astype(bf16)
-    parts = lax.all_to_all(partial, "head", split_axis=0, concat_axis=0, tiled=True)
-    layer_out = jnp.sum(
-        parts.reshape(head_count, rows, width).astype(f32), axis=0
-    ).astype(bf16)
+    partial = jnp.einsum("htd,hde->te", attn_heads, weight_heads, preferred_element_type=f32)
+    layer_out = scatter_sum(partial, "head").astype(bf16)
 
     if hi_count > 1:
         grads = lax.psum_scatter(grads, "hi", scatter_dimension=0, tiled=True).astype(bf16)

time: 282 us -> 260 us (0.922)
  waiting for transfers between devices: 148 us -> 124 us
  local copies, waits for them, and re-layouts: 12.5 us -> 22.8 us
  starting transfers between devices: 42.1 us -> 37.8 us
    ppermute x0 -> x12, waiting for transfers between devices: none -> 121 us  [swap_pieces(): lax.ppermute(send(k), axis, [(i, i ^ k) for i in range(count)])]
    all_to_all x1, waiting for transfers between devices: 56.8 us -> 0.01 us  [per_device(): lax.all_to_all(grads, ('lo', 'head'), split_axis=0, concat_axis=0, tiled=...]
    all_to_all x1, waiting for transfers between devices: 43.5 us -> 0.01 us  [per_device(): lax.all_to_all(packed, ('lo', 'head'), split_axis=0, concat_axis=0, tiled...]
    all_to_all x3 -> x0, waiting for transfers between devices: 22.4 us -> none  [the longest x1 18.8 us: per_device(): lax.all_to_all(half_sum.astype(bf16), ('hi', 'lo'), split_axis=0, concat_...]
    all_to_all x3 -> x0, starting transfers between devices: 16.7 us -> none  [the longest x1 6.76 us: per_device(): lax.all_to_all(half_sum.astype(bf16), ('hi', 'lo'), split_axis=0, concat_...]
    ppermute x0 -> x12, starting transfers between devices: none -> 14.7 us  [swap_pieces(): lax.ppermute(send(k), axis, [(i, i ^ k) for i in range(count)])]
    all_to_all x1, waiting for transfers between devices: 12.4 us -> 0.01 us  [per_device(): lax.all_to_all(attn.reshape(lo_count, range_rows, head_dim), 'lo', split_...]
    all_to_all x1, waiting for transfers between devices: 11.8 us -> 0.01 us  [per_device(): lax.all_to_all(grad_piece, 'lo', split_axis=0, concat_axis=0, tiled=True)]
  transfers between devices with their start and end apart: 10 -> 18, of which waited for: 6 -> 10; matrix products, arithmetic and copies ran while one was open for 6% -> 8% of each run, Pallas kernels for 15% -> 15%
where the time goes in v2:
time: 260 us; the launch traced here: 259 us
  waiting for transfers between devices  124 us (48%)
  Pallas kernels  39.9 us (15%)
  starting transfers between devices  37.8 us (15%)
  local copies, waits for them, and re-layouts  22.8 us (9%)
  between operations  14.2 us (5%)
  other arithmetic  11.5 us (4%)
  matrix products  9.28 us (4%)
    ppermute x12, waiting for transfers between devices, swap_pieces(): lax.ppermute(send(k), axis, [(i, i ^ k) for i in range(count)])  121 us
    pallas_call x1, Pallas kernels, per_device(): pl.pallas_call(functools.partial(backward_kernel, dims, unroll_for(block_...  22.1 us
    ppermute x12, starting transfers between devices, swap_pieces(): lax.ppermute(send(k), axis, [(i, i ^ k) for i in range(count)])  14.7 us
    pallas_call x1, Pallas kernels, per_device(): pl.pallas_call(functools.partial(forward_kernel, dims, unroll_for(block_c...  14.1 us
    unnamed x22, local copies, waits for them, and re-layouts  11.7 us
    all_to_all x1, starting transfers between devices, per_device(): lax.all_to_all(packed, ('lo', 'head'), split_axis=0, concat_axis=0, tiled...  7.24 us
    all_to_all x1, starting transfers between devices, per_device(): lax.all_to_all(attn.reshape(lo_count, range_rows, head_dim), 'lo', split_...  5.91 us
    dynamic_update_slice x4, local copies, waits for them, and re-layouts, gather_rows(): lax.dynamic_update_slice_in_dim(whole, piece, (me ^ k) * rows, axis=0)  5.72 us
  transfers between devices with their start and end apart: 18, of which 10 were waited for; matrix products, arithmetic and copies ran while one was open for 8% of the time, Pallas kernels for 15%

profile of v2, /device:TPU:16, one launch (start us, length us, event | category | flops | bytes accessed | tf_op | source)
XLA Modules:
  0.0 258.9 jit_solution(11503243351405383073)
XLA Ops:
  7.2 0.0 copy-start
  7.2 1.2 copy-done.3
  8.4 1.1 copy-done.4
  9.5 1.1 copy-done.5
  10.6 0.3 pack_heads.1
  11.0 1.3 copy-done.1
  12.2 7.2 %all-to-all-start = ((bf16[16,480,128]{2,1,0:T(8,128)(2,1)}), bf16[16,480,128]{2,1,0:T(8,128)(2,1)}, u32[]{:S(2)}, u32[]{:S(2)}) async-start(bf16[16,480,128]{2,1,0:T(8,128)(2,1)} %copy-done.1), calls=%async_computation | async-start | bytes 3932160 | tf_op jit(solution)/shard_map/all_to_all | solution.py:242
  19.5 1.5 collective-permute-start.3
  21.0 1.5 collective-permute-start.4
  22.5 0.6 collective-permute-start.5
  23.0 1.8 broadcast_in_dim.15
  24.8 0.9 constant_dynamic-update-slice_fusion.3
  25.7 21.4 %collective-permute-done.3 = bf16[160,2048]{1,0:T(8,128)(2,1)} collective-permute-done((bf16[160,2048]{1,0:T(8,128)(2,1)S(1)}, bf16[160,2048]{1,0:T(8,128)(2,1)}, u32[]{:S(2)}, u32[]{:S(2)}) %collective-permute-start.3) | collective-permute-done | bytes 655392 | tf_op jit(solution)/shard_map/ppermute | solution.py:184
  47.1 2.0 constant_dynamic-update-slice_fusion.2
  49.1 5.1 %collective-permute-done.4 = bf16[160,2048]{1,0:T(8,128)(2,1)} collective-permute-done((bf16[160,2048]{1,0:T(8,128)(2,1)S(1)}, bf16[160,2048]{1,0:T(8,128)(2,1)}, u32[]{:S(2)}, u32[]{:S(2)}) %collective-permute-start.4) | collective-permute-done | bytes 655392 | tf_op jit(solution)/shard_map/ppermute | solution.py:184
  54.1 2.0 constant_dynamic-update-slice_fusion.1
  56.1 17.9 %collective-permute-done.5 = bf16[160,2048]{1,0:T(8,128)(2,1)S(1)} collective-permute-done((bf16[160,2048]{1,0:T(8,128)(2,1)S(1)}, bf16[160,2048]{1,0:T(8,128)(2,1)S(1)}, u32[]{:S(2)}, u32[]{:S(2)}) %collective-permute-start.5) | collective-permute-done | bytes 655392 | tf_op jit(solution)/shard_map/ppermute | solution.py:184
  74.0 0.9 constant_dynamic-update-slice_fusion
  74.9 4.1 %fusion.10 = bf16[4,640,128]{2,1,0:T(8,128)(2,1)} fusion(bf16[4,128,2048]{2,1,0:T(8,128)(2,1)S(1)} %bitcast.77, bf16[640,2048]{1,0:T(8,128)(2,1)} %constant_dynamic-update-slice_fusion), kind=kOutput, calls=%fused_computation.15 | convolution fusion | flops 1342504960 | bytes 5373952 | tf_op jit(solution)/shard_map/te,hde->htd/dot_general | solution.py:257
  79.0 0.0 all-to-all-done.packed_ref
  79.0 4.2 %all-to-all-start.2 = ((bf16[4,640,128]{2,1,0:T(8,128)(2,1)}), bf16[4,640,128]{2,1,0:T(8,128)(2,1)S(1)}, u32[]{:S(2)}, u32[]{:S(2)}) async-start(bf16[4,640,128]{2,1,0:T(8,128)(2,1)} %fusion.10), calls=%async_computation.2 | async-start | bytes 1310720 | tf_op jit(solution)/shard_map/all_to_all | solution.py:261
  83.2 0.6 collective-permute-start.2
  83.8 3.3 %collective-permute-start.1 = (s32[10,4,4]{0,2,1:T(4,128)S(1)}, s32[10,4,4]{0,2,1:T(4,128)S(1)}, u32[]{:S(2)}, u32[]{:S(2)}) collective-permute-start(s32[10,4,4]{0,2,1:T(4,128)S(1)} %copy-done.10), channel_id=1, source_target_pairs={{0,8},{4,12},{8,0},{12,4},{1,9},{5,13},{9,1},{13,5},{2,10},{6,14},... | collective-permute-start | bytes 1928 | tf_op jit(solution)/shard_map/ppermute | solution.py:184
  87.0 0.0 collective-permute-start
  87.0 0.1 pad_add_fusion.1.off_ref
  87.1 10.7 %collective-permute-done.2 = s32[10,4,4]{0,2,1:T(4,128)S(1)} collective-permute-done((s32[10,4,4]{0,2,1:T(4,128)S(1)}, s32[10,4,4]{0,2,1:T(4,128)S(1)}, u32[]{:S(2)}, u32[]{:S(2)}) %collective-permute-start.2) | collective-permute-done | bytes 672 | tf_op jit(solution)/shard_map/ppermute | solution.py:184
  97.9 0.2 copy.13
  98.1 0.1 reshape.36.idx_ref
  98.2 14.1 %attention_forward.1.attn_ref = bf16[2560,128]{1,0:T(8,128)(2,1)} custom-call(s32[2]{0:T(128)S(1)} %pad_add_fusion.1.off_ref, s32[640]{0:T(1024)S(1)} %reshape.36.idx_ref, bf16[16,480,128]{2,1,0:T(8,128)(2,1)} %all-to-all-done.packed_ref), custom_call_target="tpu_custom_call" | custom-call | flops 2684354560 | bytes 2621440 | tf_op jit(solution)/shard_map/attention_forward/pallas_call | solution.py:265
  112.4 0.0 all-to-all-done.2
  112.4 5.9 %all-to-all-start.1 = ((bf16[4,640,128]{2,1,0:T(8,128)(2,1)}), bf16[4,640,128]{2,1,0:T(8,128)(2,1)S(1)}, u32[]{:S(2)}, u32[]{:S(2)}) async-start(bf16[4,640,128]{2,1,0:T(8,128)(2,1)} %bitcast.12), calls=%async_computation.1 | async-start | bytes 1310720 | tf_op jit(solution)/shard_map/all_to_all | solution.py:279
  118.3 22.1 %attention_backward.1 = bf16[16,480,128]{2,1,0:T(8,128)(2,1)S(1)} custom-call(s32[2]{0:T(128)S(1)} %pad_add_fusion.1.off_ref, s32[640]{0:T(1024)S(1)} %reshape.36.idx_ref, bf16[16,480,128]{2,1,0:T(8,128)(2,1)} %all-to-all-done.packed_ref, bf16[2560,128]{1,0:T(8,128)(2,1)} %attention_forward.1.attn_ref, bf16[2560,128]{1,0:T(8,128)(2,1)S(1)} %bitcast.78), custom_call_target="tpu_custom_call" | custom-call | flops 6710886400 | bytes 5242880 | tf_op jit(solution)/shard_map/attention_backward/pallas_call | solution.py:282
  140.3 1.4 copy-done.2
  141.7 3.6 %fusion = f32[4,128,2048]{2,1,0:T(8,128)S(1)} fusion(bf16[4,640,128]{2,1,0:T(8,128)(2,1)S(1)} %all-to-all-done.1, bf16[640,2048]{1,0:T(8,128)(2,1)} %constant_dynamic-update-slice_fusion), kind=kOutput, calls=%fused_computation.1 | convolution fusion | flops 1342177280 | bytes 7471104 | tf_op jit(solution)/shard_map/htd,te->hde/dot_general | solution.py:299
  145.3 0.0 copy-start.7
  145.3 2.0 copy-done.7
  147.3 1.1 dynamic-slice_convert_fusion
  148.4 3.0 %collective-permute-done.9 = bf16[256,2048]{1,0:T(8,128)(2,1)} collective-permute-done((bf16[256,2048]{1,0:T(8,128)(2,1)}, bf16[256,2048]{1,0:T(8,128)(2,1)}, u32[]{:S(2)}, u32[]{:S(2)}) %collective-permute-start.9) | collective-permute-done | bytes 1048608 | tf_op jit(solution)/shard_map/ppermute | solution.py:307
  151.4 2.2 convert_add_fusion
  153.6 0.0 copy-start.8
  153.6 1.3 copy-done.8
  154.9 0.8 fusion.21
  155.7 0.6 collective-permute-start.12
  156.3 3.3 %collective-permute-start.11 = (bf16[64,2048]{1,0:T(8,128)(2,1)S(1)}, bf16[64,2048]{1,0:T(8,128)(2,1)}, u32[]{:S(2)}, u32[]{:S(2)}) collective-permute-start(bf16[64,2048]{1,0:T(8,128)(2,1)S(1)} %get-tuple-element.24), channel_id=1, source_target_pairs={{0,8},{4,12},{8,0},{12,4},{1,9},{5,13},{9,1},{13,5},{2,10},{6,14},... | collective-permute-start | bytes 786440 | tf_op jit(solution)/shard_map/ppermute | solution.py:184
  159.6 0.0 collective-permute-start.10
  159.6 5.7 %all-to-all-start.3 = ((bf16[16,480,128]{2,1,0:T(8,128)(2,1)}), bf16[16,480,128]{2,1,0:T(8,128)(2,1)}, u32[]{:S(2)}, u32[]{:S(2)}) async-start(bf16[16,480,128]{2,1,0:T(8,128)(2,1)} %copy-done.2), calls=%async_computation.3 | async-start | bytes 3932160 | tf_op jit(solution)/shard_map/all_to_all | solution.py:321
  165.3 0.0 all-gather.2.cloned.1.call-start
  165.3 11.1 %collective-permute-done.12 = bf16[64,2048]{1,0:T(8,128)(2,1)} collective-permute-done((bf16[64,2048]{1,0:T(8,128)(2,1)}, bf16[64,2048]{1,0:T(8,128)(2,1)}, u32[]{:S(2)}, u32[]{:S(2)}) %collective-permute-start.12) | collective-permute-done | bytes 262176 | tf_op jit(solution)/shard_map/ppermute | solution.py:184
  176.4 14.4 %collective-permute-done.11 = bf16[64,2048]{1,0:T(8,128)(2,1)} collective-permute-done((bf16[64,2048]{1,0:T(8,128)(2,1)S(1)}, bf16[64,2048]{1,0:T(8,128)(2,1)}, u32[]{:S(2)}, u32[]{:S(2)}) %collective-permute-start.11) | collective-permute-done | bytes 262176 | tf_op jit(solution)/shard_map/ppermute | solution.py:184
  190.9 2.1 fusion.20
  193.0 0.0 all-gather.2.cloned.1.call-update
  193.1 1.5 convolution_bitcast_fusion
  194.6 2.3 copy-done.6
  197.0 1.3 fusion.13
  198.3 0.0 collective-permute-start.8
  198.3 1.6 collective-permute-start.7
  199.9 1.9 collective-permute-start.6
  201.8 22.8 %collective-permute-done.8 = bf16[160,2048]{1,0:T(8,128)(2,1)S(1)} collective-permute-done((bf16[160,2048]{1,0:T(8,128)(2,1)}, bf16[160,2048]{1,0:T(8,128)(2,1)S(1)}, u32[]{:S(2)}, u32[]{:S(2)}) %collective-permute-start.8) | collective-permute-done | bytes 655392 | tf_op jit(solution)/shard_map/ppermute | solution.py:184
  224.6 8.5 %collective-permute-done.7 = bf16[160,2048]{1,0:T(8,128)(2,1)} collective-permute-done((bf16[160,2048]{1,0:T(8,128)(2,1)}, bf16[160,2048]{1,0:T(8,128)(2,1)}, u32[]{:S(2)}, u32[]{:S(2)}) %collective-permute-start.7) | collective-permute-done | bytes 655392 | tf_op jit(solution)/shard_map/ppermute | solution.py:184
  233.1 8.5 %collective-permute-done.6 = bf16[160,2048]{1,0:T(8,128)(2,1)} collective-permute-done((bf16[160,2048]{1,0:T(8,128)(2,1)S(1)}, bf16[160,2048]{1,0:T(8,128)(2,1)}, u32[]{:S(2)}, u32[]{:S(2)}) %collective-permute-start.6) | collective-permute-done | bytes 655392 | tf_op jit(solution)/shard_map/ppermute | solution.py:184
  241.7 2.9 %fusion.16 = bf16[1,160,2048]{2,1,0:T(8,128)(2,1)} fusion(bf16[160,2048]{1,0:T(8,128)(2,1)S(1)} %collective-permute-done.8, bf16[160,2048]{1,0:T(8,128)(2,1)} %collective-permute-done.7, bf16[160,2048]{1,0:T(8,128)(2,1)} %collective-permute-done.6, f32[4,160,2048]{2,1,0:T(8,128)} %copy-done.6, s32[]{:T(128)S(6)} %select_n.46), kind=kLoop, calls=%fused_computation.19 | loop fusion | flops 2293760 | bytes 3932164 | tf_op jit(solution)/shard_map/broadcast_in_dim | solution.py:330
  244.6 0.0 all-to-all-done.3.in_ref
  244.6 3.4 %unpack_heads.1 = (bf16[160,2048]{1,0:T(8,128)(2,1)}, bf16[160,2048]{1,0:T(8,128)(2,1)}, bf16[160,2048]{1,0:T(8,128)(2,1)}) custom-call(bf16[16,480,128]{2,1,0:T(8,128)(2,1)} %all-to-all-done.3.in_ref), custom_call_target="tpu_custom_call" | custom-call | tf_op jit(solution)/shard_map/unpack_heads/pallas_call | solution.py:322
  248.0 4.1 %convert_element_type.99 = f32[512,2048]{1,0:T(8,128)} convert(bf16[512,2048]{1,0:T(8,128)(2,1)} %all-gather.2.cloned.1.call-done) | non-fusion elementwise | flops 1048576 | bytes 6291456 | tf_op jit(solution)/shard_map/convert_element_type | solution.py:314
  (18 shorter events, 0.0 us)
Async XLA Ops:
  7.2 67.7 %copy-start = (bf16[512,2048]{1,0:T(8,128)(2,1)S(1)}, bf16[512,2048]{1,0:T(8,128)(2,1)}, u32[]{:S(2)}) copy-start(bf16[512,2048]{1,0:T(8,128)(2,1)} %param.10) | copy-start | bytes 6291460
  7.2 1.2 copy-start.3
  8.4 1.1 copy-start.4
  9.5 1.1 copy-start.5
  10.9 1.3 copy-start.1
  12.2 7.2 %copy-start.9 = (bf16[1,160,2048]{2,1,0:T(8,128)(2,1)S(1)}, bf16[1,160,2048]{2,1,0:T(8,128)(2,1)}, u32[]{:S(2)}) copy-start(bf16[1,160,2048]{2,1,0:T(8,128)(2,1)} %param.11) | copy-start | bytes 1966084
  12.2 66.8 %all-to-all-start = ((bf16[16,480,128]{2,1,0:T(8,128)(2,1)}), bf16[16,480,128]{2,1,0:T(8,128)(2,1)}, u32[]{:S(2)}, u32[]{:S(2)}) async-start(bf16[16,480,128]{2,1,0:T(8,128)(2,1)} %copy-done.1), calls=%async_computation | async-start | bytes 3932160 | tf_op jit(solution)/shard_map/all_to_all | solution.py:242
  19.5 27.6 %collective-permute-start.3 = (bf16[160,2048]{1,0:T(8,128)(2,1)S(1)}, bf16[160,2048]{1,0:T(8,128)(2,1)}, u32[]{:S(2)}, u32[]{:S(2)}) collective-permute-start(bf16[160,2048]{1,0:T(8,128)(2,1)S(1)} %bitcast.87), channel_id=1, source_target_pairs={{0,1},{1,0},{2,3},{3,2},{4,5},{5,4},{6,7},{7,6},{8,9},{9,8},{10,11... | collective-permute-start | bytes 1966088 | tf_op jit(solution)/shard_map/ppermute | solution.py:184
  21.0 33.1 %collective-permute-start.4 = (bf16[160,2048]{1,0:T(8,128)(2,1)S(1)}, bf16[160,2048]{1,0:T(8,128)(2,1)}, u32[]{:S(2)}, u32[]{:S(2)}) collective-permute-start(bf16[160,2048]{1,0:T(8,128)(2,1)S(1)} %bitcast.88), channel_id=1, source_target_pairs={{0,2},{1,3},{2,0},{3,1},{4,6},{5,7},{6,4},{7,5},{8,10},{9,11},{10,... | collective-permute-start | bytes 1966088 | tf_op jit(solution)/shard_map/ppermute | solution.py:184
  22.5 51.5 %collective-permute-start.5 = (bf16[160,2048]{1,0:T(8,128)(2,1)S(1)}, bf16[160,2048]{1,0:T(8,128)(2,1)S(1)}, u32[]{:S(2)}, u32[]{:S(2)}) collective-permute-start(bf16[160,2048]{1,0:T(8,128)(2,1)S(1)} %bitcast.89), channel_id=1, source_target_pairs={{0,3},{1,2},{2,1},{3,0},{4,7},{5,6},{6,5},{7,4},{8,11},{9,10},{10,... | collective-permute-start | bytes 1966088 | tf_op jit(solution)/shard_map/ppermute | solution.py:184
  74.9 8.3 %copy-start.10 = (s32[10,4,4]{0,2,1:T(4,128)S(1)}, s32[10,4,4]{0,2,1:T(4,128)}, u32[]{:S(2)}) copy-start(s32[10,4,4]{0,2,1:T(4,128)} %param.9) | copy-start | bytes 1924
  79.0 33.3 %all-to-all-start.2 = ((bf16[4,640,128]{2,1,0:T(8,128)(2,1)}), bf16[4,640,128]{2,1,0:T(8,128)(2,1)S(1)}, u32[]{:S(2)}, u32[]{:S(2)}) async-start(bf16[4,640,128]{2,1,0:T(8,128)(2,1)} %fusion.10), calls=%async_computation.2 | async-start | bytes 1310720 | tf_op jit(solution)/shard_map/all_to_all | solution.py:261
  83.2 14.6 %collective-permute-start.2 = (s32[10,4,4]{0,2,1:T(4,128)S(1)}, s32[10,4,4]{0,2,1:T(4,128)S(1)}, u32[]{:S(2)}, u32[]{:S(2)}) collective-permute-start(s32[10,4,4]{0,2,1:T(4,128)S(1)} %copy-done.10), channel_id=1, source_target_pairs={{0,12},{4,8},{8,4},{12,0},{1,13},{5,9},{9,5},{13,1},{2,14},{6,10},... | collective-permute-start | bytes 1928 | tf_op jit(solution)/shard_map/ppermute | solution.py:184
  83.8 14.1 %collective-permute-start.1 = (s32[10,4,4]{0,2,1:T(4,128)S(1)}, s32[10,4,4]{0,2,1:T(4,128)S(1)}, u32[]{:S(2)}, u32[]{:S(2)}) collective-permute-start(s32[10,4,4]{0,2,1:T(4,128)S(1)} %copy-done.10), channel_id=1, source_target_pairs={{0,8},{4,12},{8,0},{12,4},{1,9},{5,13},{9,1},{13,5},{2,10},{6,14},... | collective-permute-start | bytes 1928 | tf_op jit(solution)/shard_map/ppermute | solution.py:184
  87.0 10.8 %collective-permute-start = (s32[10,4,4]{0,2,1:T(4,128)S(1)}, s32[10,4,4]{0,2,1:T(4,128)S(1)}, u32[]{:S(2)}, u32[]{:S(2)}) collective-permute-start(s32[10,4,4]{0,2,1:T(4,128)S(1)} %copy-done.10), channel_id=1, source_target_pairs={{0,4},{4,0},{8,12},{12,8},{1,5},{5,1},{9,13},{13,9},{2,6},{6,2},{1... | collective-permute-start | bytes 1928 | tf_op jit(solution)/shard_map/ppermute | solution.py:184
  112.4 29.3 %all-to-all-start.1 = ((bf16[4,640,128]{2,1,0:T(8,128)(2,1)}), bf16[4,640,128]{2,1,0:T(8,128)(2,1)S(1)}, u32[]{:S(2)}, u32[]{:S(2)}) async-start(bf16[4,640,128]{2,1,0:T(8,128)(2,1)} %bitcast.12), calls=%async_computation.1 | async-start | bytes 1310720 | tf_op jit(solution)/shard_map/all_to_all | solution.py:279
  140.3 1.4 copy-start.2
  145.3 2.0 copy-start.7
  148.4 3.0 %collective-permute-start.9 = (bf16[256,2048]{1,0:T(8,128)(2,1)}, bf16[256,2048]{1,0:T(8,128)(2,1)}, u32[]{:S(2)}, u32[]{:S(2)}) collective-permute-start(bf16[256,2048]{1,0:T(8,128)(2,1)} %dynamic-slice_convert_fusion), channel_id=1, source_target_pairs={{0,16},{16,0},{1,17},{17,1},{2,18},{18,2},{3,19},{19,3},{4,20},{20... | collective-permute-start | bytes 3145736 | tf_op jit(solution)/shard_map/ppermute | solution.py:307
  153.6 1.3 copy-start.8
  155.7 20.7 %collective-permute-start.12 = (bf16[64,2048]{1,0:T(8,128)(2,1)}, bf16[64,2048]{1,0:T(8,128)(2,1)}, u32[]{:S(2)}, u32[]{:S(2)}) collective-permute-start(bf16[64,2048]{1,0:T(8,128)(2,1)} %get-tuple-element.23), channel_id=1, source_target_pairs={{0,12},{4,8},{8,4},{12,0},{1,13},{5,9},{9,5},{13,1},{2,14},{6,10},... | collective-permute-start | bytes 786440 | tf_op jit(solution)/shard_map/ppermute | solution.py:184
  156.3 34.6 %collective-permute-start.11 = (bf16[64,2048]{1,0:T(8,128)(2,1)S(1)}, bf16[64,2048]{1,0:T(8,128)(2,1)}, u32[]{:S(2)}, u32[]{:S(2)}) collective-permute-start(bf16[64,2048]{1,0:T(8,128)(2,1)S(1)} %get-tuple-element.24), channel_id=1, source_target_pairs={{0,8},{4,12},{8,0},{12,4},{1,9},{5,13},{9,1},{13,5},{2,10},{6,14},... | collective-permute-start | bytes 786440 | tf_op jit(solution)/shard_map/ppermute | solution.py:184
  159.6 31.3 %collective-permute-start.10 = (bf16[64,2048]{1,0:T(8,128)(2,1)S(1)}, bf16[64,2048]{1,0:T(8,128)(2,1)}, u32[]{:S(2)}, u32[]{:S(2)}) collective-permute-start(bf16[64,2048]{1,0:T(8,128)(2,1)S(1)} %get-tuple-element.22), channel_id=1, source_target_pairs={{0,4},{4,0},{8,12},{12,8},{1,5},{5,1},{9,13},{13,9},{2,6},{6,2},{1... | collective-permute-start | bytes 786440 | tf_op jit(solution)/shard_map/ppermute | solution.py:184
  159.6 85.0 %all-to-all-start.3 = ((bf16[16,480,128]{2,1,0:T(8,128)(2,1)}), bf16[16,480,128]{2,1,0:T(8,128)(2,1)}, u32[]{:S(2)}, u32[]{:S(2)}) async-start(bf16[16,480,128]{2,1,0:T(8,128)(2,1)} %copy-done.2), calls=%async_computation.3 | async-start | bytes 3932160 | tf_op jit(solution)/shard_map/all_to_all | solution.py:321
  165.3 82.7 %all-gather.2.cloned.1.call-start = ((), (), s32[]{:S(2)}) async-start(), calls=%async_computation.4 | async-start | bytes 2359296 | tf_op jit(solution)/shard_map/all_gather | solution.py:312
  194.6 2.3 copy-start.6
  198.3 26.3 %collective-permute-start.8 = (bf16[160,2048]{1,0:T(8,128)(2,1)}, bf16[160,2048]{1,0:T(8,128)(2,1)S(1)}, u32[]{:S(2)}, u32[]{:S(2)}) collective-permute-start(bf16[160,2048]{1,0:T(8,128)(2,1)} %get-tuple-element.20), channel_id=1, source_target_pairs={{0,3},{1,2},{2,1},{3,0},{4,7},{5,6},{6,5},{7,4},{8,11},{9,10},{10,... | collective-permute-start | bytes 1966088 | tf_op jit(solution)/shard_map/ppermute | solution.py:184
  198.3 34.8 %collective-permute-start.7 = (bf16[160,2048]{1,0:T(8,128)(2,1)}, bf16[160,2048]{1,0:T(8,128)(2,1)}, u32[]{:S(2)}, u32[]{:S(2)}) collective-permute-start(bf16[160,2048]{1,0:T(8,128)(2,1)} %get-tuple-element.21), channel_id=1, source_target_pairs={{0,2},{1,3},{2,0},{3,1},{4,6},{5,7},{6,4},{7,5},{8,10},{9,11},{10,... | collective-permute-start | bytes 1966088 | tf_op jit(solution)/shard_map/ppermute | solution.py:184
  199.9 41.8 %collective-permute-start.6 = (bf16[160,2048]{1,0:T(8,128)(2,1)S(1)}, bf16[160,2048]{1,0:T(8,128)(2,1)}, u32[]{:S(2)}, u32[]{:S(2)}) collective-permute-start(bf16[160,2048]{1,0:T(8,128)(2,1)S(1)} %get-tuple-element.19), channel_id=1, source_target_pairs={{0,1},{1,0},{2,3},{3,2},{4,5},{5,4},{6,7},{7,6},{8,9},{9,8},{10,11... | collective-permute-start | bytes 1966088 | tf_op jit(solution)/shard_map/ppermute | solution.py:184
Sparse Core Ops, SparseCore 0:
  193.2 41.0 all-gather.1

commit v3 on v2

--- a/solution.py
+++ b/solution.py
@@ -75,11 +75,10 @@
 
 
 def slots_of(i, off_ref, idx_ref, dims, total):
-    lo_count, blocks, rand_count = dims
+    lo_count, rand_count = dims
     g = off_ref[0] + i
     me = off_ref[1]
-    piece = (i // blocks) ^ me
-    base = ((piece * blocks + i % blocks) * lo_count + me) * rand_count
+    base = (i * lo_count + me) * rand_count
     ids = [jnp.maximum(g - 1, 0), g, jnp.minimum(g + 1, total - 1), jnp.int32(0)]
     ids += [idx_ref[base + r] for r in range(rand_count)]
     return g, ids
@@ -242,9 +241,8 @@
     packed = lax.all_to_all(packed, ("lo", "head"), split_axis=0, concat_axis=0, tiled=True)
     if hi_count > 1:
         packed = lax.all_gather(packed, "hi", axis=0, tiled=True)
-    id_pieces = [rand_blocks] + swap_pieces(lambda k: rand_blocks, "lo")
-    ids = jnp.stack(id_pieces).reshape(-1)
-    dims = (lo_count, rand_blocks.shape[0], rand_count)
+    ids = lax.all_gather(rand_blocks, "lo", axis=0, tiled=True).reshape(-1)
+    dims = (lo_count, rand_count)
     block_count = own_rows // BLOCK_TOKENS
     offset = jnp.stack([lax.axis_index("hi") * block_count, lax.axis_index("lo")]).astype(jnp.int32)
     all_rows = own_rows * hi_count
@@ -257,11 +255,6 @@
     grad_piece = jnp.einsum(
         "te,hde->htd", cot_rows, weight_heads, preferred_element_type=f32
     ).astype(bf16)
-    packed, grad_piece = lax.optimization_barrier((packed, grad_piece))
-    grad_rows = lax.all_to_all(
-        grad_piece, "lo", split_axis=0, concat_axis=0, tiled=True
-    ).reshape(own_rows, head_dim)
-
     attn = pl.pallas_call(
         functools.partial(forward_kernel, dims, unroll_for(block_count, 4)),
         out_shape=jax.ShapeDtypeStruct((own_rows, head_dim), bf16),
@@ -279,6 +272,22 @@
     attn_heads = lax.all_to_all(
         attn.reshape(lo_count, range_rows, head_dim), "lo", split_axis=0, concat_axis=0, tiled=True
     )
+    attn_heads, grad_piece = lax.optimization_barrier((attn_heads, grad_piece))
+    grad_rows = lax.all_to_all(
+        grad_piece, "lo", split_axis=0, concat_axis=0, tiled=True
+    ).reshape(own_rows, head_dim)
+    weight_acc = jnp.einsum(
+        "htd,te->hde", attn_heads, cot_rows, preferred_element_type=f32
+    ).reshape(lo_count * head_dim, width)
+
+    half = weight_acc.shape[0] // dp_count
+    dp_index = lax.axis_index("dp")
+    own_half = lax.dynamic_slice_in_dim(weight_acc, dp_index * half, half, axis=0)
+    other_half = lax.dynamic_slice_in_dim(weight_acc, (1 - dp_index) * half, half, axis=0)
+    swapped = lax.ppermute(other_half.astype(bf16), "dp", [(0, 1), (1, 0)])
+    half_sum = own_half + swapped.astype(f32)
+    partial = jnp.einsum("htd,hde->te", attn_heads, weight_heads, preferred_element_type=f32)
+    grad_rows, half_sum, partial = lax.optimization_barrier((grad_rows, half_sum, partial))
     grads = pl.pallas_call(
         functools.partial(backward_kernel, dims, unroll_for(block_count, 4)),
         out_shape=jax.ShapeDtypeStruct(
@@ -295,25 +304,14 @@
         name="attention_backward",
     )(offset, ids, packed, attn, grad_rows)
 
-    attn_heads, grads = lax.optimization_barrier((attn_heads, grads))
-    weight_acc = jnp.einsum(
-        "htd,te->hde", attn_heads, cot_rows, preferred_element_type=f32
-    ).reshape(lo_count * head_dim, width)
-
-    half = weight_acc.shape[0] // dp_count
-    dp_index = lax.axis_index("dp")
-    own_half = lax.dynamic_slice_in_dim(weight_acc, dp_index * half, half, axis=0)
-    other_half = lax.dynamic_slice_in_dim(weight_acc, (1 - dp_index) * half, half, axis=0)
-    swapped = lax.ppermute(other_half.astype(bf16), "dp", [(0, 1), (1, 0)])
-    half_sum = own_half + swapped.astype(f32)
     token_total = dp_count * seq_count * range_rows
     ranges = "lo" if hi_count == 1 else ("hi", "lo")
     piece = scatter_sum(half_sum, ranges) * (1.0 / math.sqrt(token_total))
-    weight_grad = lax.all_gather(
-        piece.astype(bf16), ("dp", "hi", "lo"), axis=0, tiled=True
+    mine = lax.all_gather(piece.astype(bf16), ranges, axis=0, tiled=True)
+    other = lax.ppermute(mine, "dp", [(0, 1), (1, 0)])
+    weight_grad = jnp.where(
+        dp_index == 0, jnp.concatenate([mine, other]), jnp.concatenate([other, mine])
     ).astype(f32)
-
-    partial = jnp.einsum("htd,hde->te", attn_heads, weight_heads, preferred_element_type=f32)
     layer_out = scatter_sum(partial, "head").astype(bf16)
 
     if hi_count > 1:

time: 260 us -> 241 us (0.927)
  waiting for transfers between devices: 124 us -> 54 us
  blocking collectives: 0 us -> 42.8 us
    ppermute x12 -> x9, waiting for transfers between devices: 121 us -> 0.02 us  [swap_pieces(): lax.ppermute(send(k), axis, [(i, i ^ k) for i in range(count)])]
    all_gather x0 -> x1, blocking collectives: none -> 42.8 us  [per_device(): ids = lax.all_gather(rand_blocks, 'lo', axis=0, tiled=True).reshape(-1)]
    all_gather x1, waiting for transfers between devices: 0.01 us -> 39.4 us  [per_device(): mine = lax.all_gather(piece.astype(bf16), ranges, axis=0, tiled=True)]
    all_to_all x1, waiting for transfers between devices: 0.01 us -> 8.92 us  [per_device(): lax.all_to_all(grad_piece, 'lo', split_axis=0, concat_axis=0, tiled=True)]
    all_to_all x1, waiting for transfers between devices: 0.01 us -> 3.82 us  [per_device(): lax.all_to_all(grads, ('lo', 'head'), split_axis=0, concat_axis=0, tiled=...]
    convert_element_type x2, local copies, waits for them, and re-layouts: 2.14 us -> 5.73 us  [scatter_sum(): chunk_for(x, me ^ k).astype(jnp.bfloat16)]
    unnamed x22 -> x23, local copies, waits for them, and re-layouts: 11.7 us -> 8.18 us
    ppermute x1, waiting for transfers between devices: 3 us -> 0.01 us  [per_device(): swapped = lax.ppermute(other_half.astype(bf16), 'dp', [(0, 1), (1, 0)])]
  transfers between devices with their start and end apart: 18 -> 16, of which waited for: 10 -> 4; matrix products, arithmetic and copies ran while one was open for 8% -> 14% of each run, Pallas kernels for 15% -> 15%
where the time goes in v3:
time: 241 us; the launch traced here: 238 us
  waiting for transfers between devices  54 us (22%)
  blocking collectives  42.8 us (18%)
  Pallas kernels  40 us (17%)
  starting transfers between devices  39.6 us (16%)
  local copies, waits for them, and re-layouts  23.9 us (10%)
  between operations  14.2 us (6%)
  other arithmetic  12.5 us (5%)
  matrix products  10.9 us (5%)
    all_gather x1, blocking collectives, per_device(): ids = lax.all_gather(rand_blocks, 'lo', axis=0, tiled=True).reshape(-1)  42.8 us
    all_gather x1, waiting for transfers between devices, per_device(): mine = lax.all_gather(piece.astype(bf16), ranges, axis=0, tiled=True)  39.4 us
    pallas_call x1, Pallas kernels, per_device(): pl.pallas_call(functools.partial(backward_kernel, dims, unroll_for(block_...  22.3 us
    pallas_call x1, Pallas kernels, per_device(): pl.pallas_call(functools.partial(forward_kernel, dims, unroll_for(block_c...  14 us
    ppermute x9, starting transfers between devices, swap_pieces(): lax.ppermute(send(k), axis, [(i, i ^ k) for i in range(count)])  11.8 us
    all_to_all x1, waiting for transfers between devices, per_device(): lax.all_to_all(grad_piece, 'lo', split_axis=0, concat_axis=0, tiled=True)  8.92 us
    unnamed x23, local copies, waits for them, and re-layouts  8.18 us
    all_to_all x1, starting transfers between devices, per_device(): lax.all_to_all(grads, ('lo', 'head'), split_axis=0, concat_axis=0, tiled=...  7.87 us
  transfers between devices with their start and end apart: 16, of which 4 were waited for; matrix products, arithmetic and copies ran while one was open for 14% of the time, Pallas kernels for 15%

profile of v3, /device:TPU:16, one launch (start us, length us, event | category | flops | bytes accessed | tf_op | source)
XLA Modules:
  0.0 238.0 jit_solution(6295503176023728098)
XLA Ops:
  7.2 0.0 copy-start
  7.2 1.2 copy-done.3
  8.4 1.1 copy-done.4
  9.5 1.1 copy-done.5
  10.6 0.3 pack_heads.1
  11.0 1.3 copy-done.1
  12.2 7.2 %all-to-all-start = ((bf16[16,480,128]{2,1,0:T(8,128)(2,1)}), bf16[16,480,128]{2,1,0:T(8,128)(2,1)}, u32[]{:S(2)}, u32[]{:S(2)}) async-start(bf16[16,480,128]{2,1,0:T(8,128)(2,1)} %copy-done.1), calls=%async_computation | async-start | bytes 3932160 | tf_op jit(solution)/shard_map/all_to_all | solution.py:241
  19.5 1.5 collective-permute-start.1
  21.0 1.5 collective-permute-start
  22.5 0.6 collective-permute-start.2
  23.1 1.8 broadcast_in_dim.15
  24.9 0.9 constant_dynamic-update-slice_fusion.3
  25.8 0.1 copy.14
  25.9 42.8 %all_gather.6 = s32[40,4,4]{2,1,0:T(4,128)S(1)} all-gather(s32[10,4,4]{2,1,0:T(4,128)S(1)} %copy.14), channel_id=1, replica_groups=mesh['dp'=2,'seq'=4,'head'=4] {'seq'}, dimensions={0}, use_global_device_ids=true | all-gather | bytes 3200 | tf_op jit(solution)/shard_map/all_gather | solution.py:244
  68.7 0.1 reshape.37.idx_ref
  68.8 0.1 pad_add_fusion.off_ref
  68.9 0.0 all-to-all-done.packed_ref
  68.9 14.0 %attention_forward.1.attn_ref = bf16[2560,128]{1,0:T(8,128)(2,1)} custom-call(s32[2]{0:T(128)S(1)} %pad_add_fusion.off_ref, s32[640]{0:T(1024)S(1)} %reshape.37.idx_ref, bf16[16,480,128]{2,1,0:T(8,128)(2,1)} %all-to-all-done.packed_ref), custom_call_target="tpu_custom_call" | custom-call | flops 2684354560 | bytes 2621440 | tf_op jit(solution)/shard_map/attention_forward/pallas_call | solution.py:258
  82.9 5.9 %all-to-all-start.1 = ((bf16[4,640,128]{2,1,0:T(8,128)(2,1)}), bf16[4,640,128]{2,1,0:T(8,128)(2,1)S(1)}, u32[]{:S(2)}, u32[]{:S(2)}) async-start(bf16[4,640,128]{2,1,0:T(8,128)(2,1)} %bitcast.4), calls=%async_computation.1 | async-start | bytes 1310720 | tf_op jit(solution)/shard_map/all_to_all | solution.py:272
  88.8 0.0 collective-permute-done
  88.8 2.0 constant_dynamic-update-slice_fusion.2
  90.8 0.0 collective-permute-done.1
  90.8 2.0 constant_dynamic-update-slice_fusion.1
  92.8 0.0 collective-permute-done.2
  92.8 2.0 constant_dynamic-update-slice_fusion
  94.8 4.1 %fusion.11 = bf16[4,640,128]{2,1,0:T(8,128)(2,1)} fusion(bf16[4,128,2048]{2,1,0:T(8,128)(2,1)S(1)} %bitcast.66, bf16[640,2048]{1,0:T(8,128)(2,1)} %constant_dynamic-update-slice_fusion), kind=kOutput, calls=%fused_computation.17 | convolution fusion | flops 1342504960 | bytes 5373952 | tf_op jit(solution)/shard_map/te,hde->htd/dot_general | solution.py:255
  98.9 1.8 all-to-all-done.1
  100.7 3.6 %fusion = f32[4,128,2048]{2,1,0:T(8,128)S(1)} fusion(bf16[4,640,128]{2,1,0:T(8,128)(2,1)S(1)} %all-to-all-done.1, bf16[640,2048]{1,0:T(8,128)(2,1)} %constant_dynamic-update-slice_fusion), kind=kOutput, calls=%fused_computation.1 | convolution fusion | flops 1342177280 | bytes 7471104 | tf_op jit(solution)/shard_map/htd,te->hde/dot_general | solution.py:279
  104.3 0.0 copy-start.6
  104.3 2.0 copy-done.6
  106.3 1.2 dynamic-slice_convert_fusion
  107.6 0.0 collective-permute-start.3
  107.6 6.7 %all-to-all-start.2 = ((bf16[4,640,128]{2,1,0:T(8,128)(2,1)}), bf16[4,640,128]{2,1,0:T(8,128)(2,1)S(1)}, u32[]{:S(2)}, u32[]{:S(2)}) async-start(bf16[4,640,128]{2,1,0:T(8,128)(2,1)} %fusion.11), calls=%async_computation.2 | async-start | bytes 1310720 | tf_op jit(solution)/shard_map/all_to_all | solution.py:276
  114.3 3.2 %convolution_bitcast_fusion = f32[640,2048]{1,0:T(8,128)} fusion(bf16[4,640,128]{2,1,0:T(8,128)(2,1)S(1)} %all-to-all-done.1, bf16[4,128,2048]{2,1,0:T(8,128)(2,1)S(1)} %bitcast.67), kind=kOutput, calls=%fused_computation | convolution fusion | flops 1342177280 | bytes 7995392 | tf_op jit(solution)/shard_map/htd,hde->te/dot_general | solution.py:289
  117.5 0.0 collective-permute-done.3
  117.5 2.8 %convert_add_fusion = f32[256,2048]{1,0:T(8,128)} fusion(bf16[256,2048]{1,0:T(8,128)(2,1)} %collective-permute-done.3, f32[512,2048]{1,0:T(8,128)S(1)} %bitcast.73, s32[]{:T(128)S(6)} %select_n.54), kind=kLoop, calls=%fused_computation.7 | loop fusion | flops 1048576 | bytes 5242884 | tf_op jit(solution)/shard_map/add | solution.py:288
  120.4 8.9 %all-to-all-done.2 = bf16[4,640,128]{2,1,0:T(8,128)(2,1)S(1)} async-done(((bf16[4,640,128]{2,1,0:T(8,128)(2,1)}), bf16[4,640,128]{2,1,0:T(8,128)(2,1)S(1)}, u32[]{:S(2)}, u32[]{:S(2)}) %all-to-all-start.2) | async-done | bytes 655392 | tf_op jit(solution)/shard_map/all_to_all | solution.py:276
  129.3 2.3 fusion.22
  131.5 2.4 collective-permute-start.7
  133.9 1.5 collective-permute-start.9
  135.4 0.9 collective-permute-start.8
  136.3 22.3 %attention_backward.1 = bf16[16,480,128]{2,1,0:T(8,128)(2,1)S(1)} custom-call(s32[2]{0:T(128)S(1)} %pad_add_fusion.off_ref, s32[640]{0:T(1024)S(1)} %reshape.37.idx_ref, bf16[16,480,128]{2,1,0:T(8,128)(2,1)} %all-to-all-done.packed_ref, bf16[2560,128]{1,0:T(8,128)(2,1)} %attention_forward.1.attn_ref, bf16[2560,128]{1,0:T(8,128)(2,1)S(1)} %bitcast.68), custom_call_target="tpu_custom_call" | custom-call | flops 6710886400 | bytes 5242880 | tf_op jit(solution)/shard_map/attention_backward/pallas_call | solution.py:291
  158.6 1.3 copy-done.2
  160.0 7.9 %all-to-all-start.3 = ((bf16[16,480,128]{2,1,0:T(8,128)(2,1)}), bf16[16,480,128]{2,1,0:T(8,128)(2,1)}, u32[]{:S(2)}, u32[]{:S(2)}) async-start(bf16[16,480,128]{2,1,0:T(8,128)(2,1)} %copy-done.2), calls=%async_computation.3 | async-start | bytes 3932160 | tf_op jit(solution)/shard_map/all_to_all | solution.py:319
  167.8 0.0 all-gather.2.cloned.1.call-start
  167.9 0.0 collective-permute-done.7
  167.9 0.0 collective-permute-done.9
  167.9 0.0 collective-permute-done.8
  167.9 2.1 fusion.21
  170.0 0.0 all-gather.2.cloned.1.call-update
  170.1 3.5 %fusion.14 = (bf16[160,2048]{1,0:T(8,128)(2,1)}, bf16[160,2048]{1,0:T(8,128)(2,1)}, bf16[160,2048]{1,0:T(8,128)(2,1)}) fusion(f32[4,160,2048]{2,1,0:T(8,128)} %bitcast.76, s32[]{:T(128)S(6)} %select_n.57, s32[]{:T(128)S(6)} %select_n.59, s32[]{:T(128)S(6)} %select_n.58), kind=kLoop, calls=%fused_computation.18 | loop fusion | bytes 3932172 | tf_op jit(solution)/shard_map/convert_element_type | solution.py:201
  173.5 1.5 collective-permute-start.4
  175.0 1.5 collective-permute-start.6
  176.5 0.6 collective-permute-start.5
  177.0 39.4 %all-gather.2.cloned.1.call-done = bf16[256,2048]{1,0:T(8,128)(2,1)} async-done(((bf16[64,2048]{1,0:T(8,128)(2,1)}), bf16[256,2048]{1,0:T(8,128)(2,1)}) %all-gather.2.cloned.1.call-update) | async-done | bytes 1048592 | tf_op jit(solution)/shard_map/all_gather | solution.py:310
  216.4 0.1 collective-permute-start.10
  216.5 0.0 collective-permute-done.4
  216.5 0.0 collective-permute-done.6
  216.5 0.0 collective-permute-done.5
  216.5 3.2 %fusion.17 = bf16[1,160,2048]{2,1,0:T(8,128)(2,1)} fusion(bf16[160,2048]{1,0:T(8,128)(2,1)} %collective-permute-done.6, bf16[160,2048]{1,0:T(8,128)(2,1)} %collective-permute-done.5, bf16[160,2048]{1,0:T(8,128)(2,1)} %collective-permute-done.4, f32[4,160,2048]{2,1,0:T(8,128)} %bitcast.77, s32[]{:T(128)S(6)} %select_n.56), kind=kLoop, calls=%fused_computation.21 | loop fusion | flops 2293760 | bytes 3932164 | tf_op jit(solution)/shard_map/broadcast_in_dim | solution.py:328
  219.7 0.0 collective-permute-done.10
  219.7 4.2 %fusion.4 = f32[512,2048]{1,0:T(8,128)} fusion(bf16[256,2048]{1,0:T(8,128)(2,1)} %collective-permute-done.10, bf16[256,2048]{1,0:T(8,128)(2,1)S(1)} %copy-done.8, pred[]{:T(512)S(6)} %eq.3), kind=kLoop, calls=%fused_computation.6 | loop fusion | flops 10485760 | bytes 6291457 | tf_op jit(solution)/shard_map/convert_element_type | solution.py:314
  223.9 3.8 %all-to-all-done.3.in_ref = bf16[16,480,128]{2,1,0:T(8,128)(2,1)} async-done(((bf16[16,480,128]{2,1,0:T(8,128)(2,1)}), bf16[16,480,128]{2,1,0:T(8,128)(2,1)}, u32[]{:S(2)}, u32[]{:S(2)}) %all-to-all-start.3) | async-done | bytes 1966112 | tf_op jit(solution)/shard_map/all_to_all | solution.py:319
  227.8 3.4 %unpack_heads.1 = (bf16[160,2048]{1,0:T(8,128)(2,1)}, bf16[160,2048]{1,0:T(8,128)(2,1)}, bf16[160,2048]{1,0:T(8,128)(2,1)}) custom-call(bf16[16,480,128]{2,1,0:T(8,128)(2,1)} %all-to-all-done.3.in_ref), custom_call_target="tpu_custom_call" | custom-call | tf_op jit(solution)/shard_map/unpack_heads/pallas_call | solution.py:320
  (14 shorter events, 0.0 us)
Async XLA Ops:
  7.2 87.6 %copy-start = (bf16[512,2048]{1,0:T(8,128)(2,1)S(1)}, bf16[512,2048]{1,0:T(8,128)(2,1)}, u32[]{:S(2)}) copy-start(bf16[512,2048]{1,0:T(8,128)(2,1)} %param.10) | copy-start | bytes 6291460
  7.2 1.2 copy-start.3
  8.4 1.1 copy-start.4
  9.5 1.1 copy-start.5
  10.9 1.3 copy-start.1
  12.2 7.3 %copy-start.9 = (bf16[1,160,2048]{2,1,0:T(8,128)(2,1)S(1)}, bf16[1,160,2048]{2,1,0:T(8,128)(2,1)}, u32[]{:S(2)}) copy-start(bf16[1,160,2048]{2,1,0:T(8,128)(2,1)} %param.11) | copy-start | bytes 1966084
  12.2 56.7 %all-to-all-start = ((bf16[16,480,128]{2,1,0:T(8,128)(2,1)}), bf16[16,480,128]{2,1,0:T(8,128)(2,1)}, u32[]{:S(2)}, u32[]{:S(2)}) async-start(bf16[16,480,128]{2,1,0:T(8,128)(2,1)} %copy-done.1), calls=%async_computation | async-start | bytes 3932160 | tf_op jit(solution)/shard_map/all_to_all | solution.py:241
  19.5 6.3 %copy-start.10 = (s32[10,4,4]{0,2,1:T(4,128)S(1)}, s32[10,4,4]{0,2,1:T(4,128)}, u32[]{:S(2)}) copy-start(s32[10,4,4]{0,2,1:T(4,128)} %param.9) | copy-start | bytes 1924
  19.5 71.3 %collective-permute-start.1 = (bf16[160,2048]{1,0:T(8,128)(2,1)S(1)}, bf16[160,2048]{1,0:T(8,128)(2,1)}, u32[]{:S(2)}, u32[]{:S(2)}) collective-permute-start(bf16[160,2048]{1,0:T(8,128)(2,1)S(1)} %bitcast.78), channel_id=1, source_target_pairs={{0,2},{1,3},{2,0},{3,1},{4,6},{5,7},{6,4},{7,5},{8,10},{9,11},{10,... | collective-permute-start | bytes 1966088 | tf_op jit(solution)/shard_map/ppermute | solution.py:183
  21.0 67.8 %collective-permute-start = (bf16[160,2048]{1,0:T(8,128)(2,1)S(1)}, bf16[160,2048]{1,0:T(8,128)(2,1)}, u32[]{:S(2)}, u32[]{:S(2)}) collective-permute-start(bf16[160,2048]{1,0:T(8,128)(2,1)S(1)} %bitcast.79), channel_id=1, source_target_pairs={{0,1},{1,0},{2,3},{3,2},{4,5},{5,4},{6,7},{7,6},{8,9},{9,8},{10,11... | collective-permute-start | bytes 1966088 | tf_op jit(solution)/shard_map/ppermute | solution.py:183
  22.5 70.3 %collective-permute-start.2 = (bf16[160,2048]{1,0:T(8,128)(2,1)S(1)}, bf16[160,2048]{1,0:T(8,128)(2,1)}, u32[]{:S(2)}, u32[]{:S(2)}) collective-permute-start(bf16[160,2048]{1,0:T(8,128)(2,1)S(1)} %bitcast.80), channel_id=1, source_target_pairs={{0,3},{1,2},{2,1},{3,0},{4,7},{5,6},{6,5},{7,4},{8,11},{9,10},{10,... | collective-permute-start | bytes 1966088 | tf_op jit(solution)/shard_map/ppermute | solution.py:183
  82.9 17.8 %all-to-all-start.1 = ((bf16[4,640,128]{2,1,0:T(8,128)(2,1)}), bf16[4,640,128]{2,1,0:T(8,128)(2,1)S(1)}, u32[]{:S(2)}, u32[]{:S(2)}) async-start(bf16[4,640,128]{2,1,0:T(8,128)(2,1)} %bitcast.4), calls=%async_computation.1 | async-start | bytes 1310720 | tf_op jit(solution)/shard_map/all_to_all | solution.py:272
  104.3 2.0 copy-start.6
  107.6 10.0 %collective-permute-start.3 = (bf16[256,2048]{1,0:T(8,128)(2,1)}, bf16[256,2048]{1,0:T(8,128)(2,1)}, u32[]{:S(2)}, u32[]{:S(2)}) collective-permute-start(bf16[256,2048]{1,0:T(8,128)(2,1)} %dynamic-slice_convert_fusion), channel_id=1, source_target_pairs={{0,16},{16,0},{1,17},{17,1},{2,18},{18,2},{3,19},{19,3},{4,20},{20... | collective-permute-start | bytes 3145736 | tf_op jit(solution)/shard_map/ppermute | solution.py:287
  107.6 21.7 %all-to-all-start.2 = ((bf16[4,640,128]{2,1,0:T(8,128)(2,1)}), bf16[4,640,128]{2,1,0:T(8,128)(2,1)S(1)}, u32[]{:S(2)}, u32[]{:S(2)}) async-start(bf16[4,640,128]{2,1,0:T(8,128)(2,1)} %fusion.11), calls=%async_computation.2 | async-start | bytes 1310720 | tf_op jit(solution)/shard_map/all_to_all | solution.py:276
  114.3 3.2 %copy-start.7 = (f32[4,128,2048]{2,1,0:T(8,128)S(1)}, f32[4,128,2048]{2,1,0:T(8,128)}, u32[]{:S(2)}) copy-start(f32[4,128,2048]{2,1,0:T(8,128)} %copy-done.6) | copy-start | bytes 12582916
  131.5 36.3 %collective-permute-start.7 = (bf16[64,2048]{1,0:T(8,128)(2,1)}, bf16[64,2048]{1,0:T(8,128)(2,1)}, u32[]{:S(2)}, u32[]{:S(2)}) collective-permute-start(bf16[64,2048]{1,0:T(8,128)(2,1)} %get-tuple-element.24), channel_id=1, source_target_pairs={{0,4},{4,0},{8,12},{12,8},{1,5},{5,1},{9,13},{13,9},{2,6},{6,2},{1... | collective-permute-start | bytes 786440 | tf_op jit(solution)/shard_map/ppermute | solution.py:183
  133.9 34.0 %collective-permute-start.9 = (bf16[64,2048]{1,0:T(8,128)(2,1)}, bf16[64,2048]{1,0:T(8,128)(2,1)}, u32[]{:S(2)}, u32[]{:S(2)}) collective-permute-start(bf16[64,2048]{1,0:T(8,128)(2,1)} %get-tuple-element.25), channel_id=1, source_target_pairs={{0,12},{4,8},{8,4},{12,0},{1,13},{5,9},{9,5},{13,1},{2,14},{6,10},... | collective-permute-start | bytes 786440 | tf_op jit(solution)/shard_map/ppermute | solution.py:183
  135.4 32.5 %collective-permute-start.8 = (bf16[64,2048]{1,0:T(8,128)(2,1)}, bf16[64,2048]{1,0:T(8,128)(2,1)}, u32[]{:S(2)}, u32[]{:S(2)}) collective-permute-start(bf16[64,2048]{1,0:T(8,128)(2,1)} %get-tuple-element.26), channel_id=1, source_target_pairs={{0,8},{4,12},{8,0},{12,4},{1,9},{5,13},{9,1},{13,5},{2,10},{6,14},... | collective-permute-start | bytes 786440 | tf_op jit(solution)/shard_map/ppermute | solution.py:183
  158.6 1.4 copy-start.2
  160.0 67.8 %all-to-all-start.3 = ((bf16[16,480,128]{2,1,0:T(8,128)(2,1)}), bf16[16,480,128]{2,1,0:T(8,128)(2,1)}, u32[]{:S(2)}, u32[]{:S(2)}) async-start(bf16[16,480,128]{2,1,0:T(8,128)(2,1)} %copy-done.2), calls=%async_computation.3 | async-start | bytes 3932160 | tf_op jit(solution)/shard_map/all_to_all | solution.py:319
  167.8 48.6 %all-gather.2.cloned.1.call-start = ((), (), s32[]{:S(2)}) async-start(), calls=%async_computation.4 | async-start | bytes 1310720 | tf_op jit(solution)/shard_map/all_gather | solution.py:310
  173.5 43.0 %collective-permute-start.4 = (bf16[160,2048]{1,0:T(8,128)(2,1)}, bf16[160,2048]{1,0:T(8,128)(2,1)}, u32[]{:S(2)}, u32[]{:S(2)}) collective-permute-start(bf16[160,2048]{1,0:T(8,128)(2,1)} %get-tuple-element.21), channel_id=1, source_target_pairs={{0,1},{1,0},{2,3},{3,2},{4,5},{5,4},{6,7},{7,6},{8,9},{9,8},{10,11... | collective-permute-start | bytes 1966088 | tf_op jit(solution)/shard_map/ppermute | solution.py:183
  175.0 41.5 %collective-permute-start.6 = (bf16[160,2048]{1,0:T(8,128)(2,1)}, bf16[160,2048]{1,0:T(8,128)(2,1)}, u32[]{:S(2)}, u32[]{:S(2)}) collective-permute-start(bf16[160,2048]{1,0:T(8,128)(2,1)} %get-tuple-element.22), channel_id=1, source_target_pairs={{0,3},{1,2},{2,1},{3,0},{4,7},{5,6},{6,5},{7,4},{8,11},{9,10},{10,... | collective-permute-start | bytes 1966088 | tf_op jit(solution)/shard_map/ppermute | solution.py:183
  176.5 40.0 %collective-permute-start.5 = (bf16[160,2048]{1,0:T(8,128)(2,1)}, bf16[160,2048]{1,0:T(8,128)(2,1)}, u32[]{:S(2)}, u32[]{:S(2)}) collective-permute-start(bf16[160,2048]{1,0:T(8,128)(2,1)} %get-tuple-element.23), channel_id=1, source_target_pairs={{0,2},{1,3},{2,0},{3,1},{4,6},{5,7},{6,4},{7,5},{8,10},{9,11},{10,... | collective-permute-start | bytes 1966088 | tf_op jit(solution)/shard_map/ppermute | solution.py:183
  216.4 3.3 %copy-start.8 = (bf16[256,2048]{1,0:T(8,128)(2,1)S(1)}, bf16[256,2048]{1,0:T(8,128)(2,1)}, u32[]{:S(2)}) copy-start(bf16[256,2048]{1,0:T(8,128)(2,1)} %all-gather.2.cloned.1.call-done) | copy-start | bytes 3145732
  216.4 3.3 %collective-permute-start.10 = (bf16[256,2048]{1,0:T(8,128)(2,1)}, bf16[256,2048]{1,0:T(8,128)(2,1)}, u32[]{:S(2)}, u32[]{:S(2)}) collective-permute-start(bf16[256,2048]{1,0:T(8,128)(2,1)} %all-gather.2.cloned.1.call-done), channel_id=1, source_target_pairs={{0,16},{16,0},{1,17},{17,1},{2,18},{18,2},{3,19},{19,3},{4,20},{20... | collective-permute-start | bytes 3145736 | tf_op jit(solution)/shard_map/ppermute | solution.py:311
Sparse Core Ops, SparseCore 0:
  170.8 45.5 all-gather.1

commit v4 on v3

--- a/solution.py
+++ b/solution.py
@@ -75,10 +75,11 @@
 
 
 def slots_of(i, off_ref, idx_ref, dims, total):
-    lo_count, rand_count = dims
+    lo_count, blocks, rand_count = dims
     g = off_ref[0] + i
     me = off_ref[1]
-    base = (i * lo_count + me) * rand_count
+    piece = (i // blocks) ^ me
+    base = ((piece * blocks + i % blocks) * lo_count + me) * rand_count
     ids = [jnp.maximum(g - 1, 0), g, jnp.minimum(g + 1, total - 1), jnp.int32(0)]
     ids += [idx_ref[base + r] for r in range(rand_count)]
     return g, ids
@@ -177,10 +178,11 @@
     return max(u for u in range(1, most + 1) if count % u == 0)
 
 
-def swap_pieces(send, axis):
+def swap_pieces(pieces, axis):
     count = lax.axis_size(axis)
     return [
-        lax.ppermute(send(k), axis, [(i, i ^ k) for i in range(count)]) for k in range(1, count)
+        lax.ppermute(piece, axis, [(i, i ^ k) for i in range(count)])
+        for k, piece in enumerate(pieces, 1)
     ]
 
 
@@ -188,28 +190,25 @@
     return lax.dynamic_slice_in_dim(x, index, 1, axis=0)[0]
 
 
-def scatter_sum(x, axis):
+def cut_terms(x, axis):
     count = lax.axis_size(axis)
     me = lax.axis_index(axis)
     x = x.reshape((count, x.shape[0] // count) + x.shape[1:])
     if count > 4:
-        pieces = lax.all_to_all(
-            x.astype(jnp.bfloat16), axis, split_axis=0, concat_axis=0, tiled=True
-        )
+        return (x.astype(jnp.bfloat16),)
+    return (chunk_for(x, me),) + tuple(
+        chunk_for(x, me ^ k).astype(jnp.bfloat16) for k in range(1, count)
+    )
+
+
+def sum_terms(terms, axis):
+    if len(terms) == 1:
+        pieces = lax.all_to_all(terms[0], axis, split_axis=0, concat_axis=0, tiled=True)
         return jnp.sum(pieces.astype(jnp.float32), axis=0)
-    total = chunk_for(x, me).astype(jnp.float32)
-    for piece in swap_pieces(lambda k: chunk_for(x, me ^ k).astype(jnp.bfloat16), axis):
+    total = terms[0].astype(jnp.float32)
+    for piece in swap_pieces(terms[1:], axis):
         total = total + piece.astype(jnp.float32)
     return total
-
-
-def gather_rows(x, axis):
-    rows = x.shape[0]
-    me = lax.axis_index(axis)
-    whole = jnp.zeros((rows * lax.axis_size(axis),) + x.shape[1:], x.dtype)
-    for k, piece in enumerate([x] + swap_pieces(lambda k: x, axis)):
-        whole = lax.dynamic_update_slice_in_dim(whole, piece, (me ^ k) * rows, axis=0)
-    return whole
 
 
 def params():
@@ -241,8 +240,9 @@
     packed = lax.all_to_all(packed, ("lo", "head"), split_axis=0, concat_axis=0, tiled=True)
     if hi_count > 1:
         packed = lax.all_gather(packed, "hi", axis=0, tiled=True)
-    ids = lax.all_gather(rand_blocks, "lo", axis=0, tiled=True).reshape(-1)
-    dims = (lo_count, rand_count)
+    id_pieces = [rand_blocks] + swap_pieces([rand_blocks] * (lo_count - 1), "lo")
+    ids = jnp.stack(id_pieces).reshape(-1)
+    dims = (lo_count, rand_blocks.shape[0], rand_count)
     block_count = own_rows // BLOCK_TOKENS
     offset = jnp.stack([lax.axis_index("hi") * block_count, lax.axis_index("lo")]).astype(jnp.int32)
     all_rows = own_rows * hi_count
@@ -250,7 +250,7 @@
     summed = pltpu.VMEM((all_rows, head_dim), f32)
     pair = 2 * own_rows * 8 * BLOCK_TOKENS * head_dim
 
-    cot_rows = gather_rows(cotangent[0], "head")
+    cot_rows = lax.all_gather(cotangent[0], "head", axis=0, tiled=True)
     weight_heads = out_weight.reshape(lo_count, head_dim, width)
     grad_piece = jnp.einsum(
         "te,hde->htd", cot_rows, weight_heads, preferred_element_type=f32
@@ -287,7 +287,12 @@
     swapped = lax.ppermute(other_half.astype(bf16), "dp", [(0, 1), (1, 0)])
     half_sum = own_half + swapped.astype(f32)
     partial = jnp.einsum("htd,hde->te", attn_heads, weight_heads, preferred_element_type=f32)
-    grad_rows, half_sum, partial = lax.optimization_barrier((grad_rows, half_sum, partial))
+    ranges = "lo" if hi_count == 1 else ("hi", "lo")
+    weight_terms = cut_terms(half_sum, ranges)
+    out_terms = cut_terms(partial, "head")
+    grad_rows, weight_terms, out_terms = lax.optimization_barrier(
+        (grad_rows, weight_terms, out_terms)
+    )
     grads = pl.pallas_call(
         functools.partial(backward_kernel, dims, unroll_for(block_count, 4)),
         out_shape=jax.ShapeDtypeStruct(
@@ -305,14 +310,13 @@
     )(offset, ids, packed, attn, grad_rows)
 
     token_total = dp_count * seq_count * range_rows
-    ranges = "lo" if hi_count == 1 else ("hi", "lo")
-    piece = scatter_sum(half_sum, ranges) * (1.0 / math.sqrt(token_total))
+    piece = sum_terms(weight_terms, ranges) * (1.0 / math.sqrt(token_total))
     mine = lax.all_gather(piece.astype(bf16), ranges, axis=0, tiled=True)
     other = lax.ppermute(mine, "dp", [(0, 1), (1, 0)])
     weight_grad = jnp.where(
         dp_index == 0, jnp.concatenate([mine, other]), jnp.concatenate([other, mine])
     ).astype(f32)
-    layer_out = scatter_sum(partial, "head").astype(bf16)
+    layer_out = sum_terms(out_terms, "head").astype(bf16)
 
     if hi_count > 1:
         grads = lax.psum_scatter(grads, "hi", scatter_dimension=0, tiled=True).astype(bf16)

time: 241 us -> 239 us (level)
  waiting for transfers between devices: 54 us -> 107 us
  blocking collectives: 42.8 us -> 0 us
  local copies, waits for them, and re-layouts: 23.9 us -> 14 us
    all_gather x1 -> x0, blocking collectives: 42.8 us -> none  [per_device(): ids = lax.all_gather(rand_blocks, 'lo', axis=0, tiled=True).reshape(-1)]
    ppermute x9, waiting for transfers between devices: 0.02 us -> 38.6 us  [swap_pieces(): lax.ppermute(piece, axis, [(i, i ^ k) for i in range(count)])]
    all_to_all x1, waiting for transfers between devices: 1.84 us -> 8.87 us  [per_device(): lax.all_to_all(attn.reshape(lo_count, range_rows, head_dim), 'lo', split_...]
    dynamic_update_slice x4 -> x0, local copies, waits for them, and re-layouts: 6.83 us -> none  [gather_rows(): lax.dynamic_update_slice_in_dim(whole, piece, (me ^ k) * rows, axis=0)]
    all_gather x1, waiting for transfers between devices: 39.4 us -> 42.8 us  [per_device(): mine = lax.all_gather(piece.astype(bf16), ranges, axis=0, tiled=True)]
    convert_element_type x2, local copies, waits for them, and re-layouts: 5.73 us -> 2.28 us  [cut_terms(): chunk_for(x, me ^ k).astype(jnp.bfloat16)]
    unnamed x23 -> x20, local copies, waits for them, and re-layouts: 8.18 us -> 7.96 us
  transfers between devices with their start and end apart: 16 -> 17, of which waited for: 4 -> 8; matrix products, arithmetic and copies ran while one was open for 14% -> 8% of each run, Pallas kernels for 15% -> 15%
where the time goes in v4:
time: 239 us; the launch traced here: 236 us
  waiting for transfers between devices  107 us (45%)
  Pallas kernels  39.9 us (17%)
  starting transfers between devices  39.4 us (16%)
  between operations  14.2 us (6%)
  local copies, waits for them, and re-layouts  14 us (6%)
  other arithmetic  11.4 us (5%)
  matrix products  9.54 us (4%)
    all_gather x1, waiting for transfers between devices, per_device(): mine = lax.all_gather(piece.astype(bf16), ranges, axis=0, tiled=True)  42.8 us
    ppermute x9, waiting for transfers between devices, swap_pieces(): lax.ppermute(piece, axis, [(i, i ^ k) for i in range(count)])  38.6 us
    pallas_call x1, Pallas kernels, per_device(): pl.pallas_call(functools.partial(backward_kernel, dims, unroll_for(block_...  22.1 us
    pallas_call x1, Pallas kernels, per_device(): pl.pallas_call(functools.partial(forward_kernel, dims, unroll_for(block_c...  14.2 us
    ppermute x9, starting transfers between devices, swap_pieces(): lax.ppermute(piece, axis, [(i, i ^ k) for i in range(count)])  11.8 us
    all_to_all x1, waiting for transfers between devices, per_device(): lax.all_to_all(grad_piece, 'lo', split_axis=0, concat_axis=0, tiled=True)  10.9 us
    all_to_all x1, starting transfers between devices, per_device(): lax.all_to_all(grads, ('lo', 'head'), split_axis=0, concat_axis=0, tiled=...  8.96 us
    all_to_all x1, waiting for transfers between devices, per_device(): lax.all_to_all(attn.reshape(lo_count, range_rows, head_dim), 'lo', split_...  8.87 us
  transfers between devices with their start and end apart: 17, of which 8 were waited for; matrix products, arithmetic and copies ran while one was open for 8% of the time, Pallas kernels for 15%

profile of v4, /device:TPU:16, one launch (start us, length us, event | category | flops | bytes accessed | tf_op | source)
XLA Modules:
  0.0 236.0 jit_solution(14641525147841890265)
XLA Ops:
  7.2 0.0 copy-start
  7.2 1.2 copy-done.3
  8.4 1.1 copy-done.4
  9.5 1.1 copy-done.5
  10.6 0.3 pack_heads.1
  10.9 0.0 copy-start.1
  11.0 1.3 copy-done.1
  12.2 7.2 %all-to-all-start = ((bf16[16,480,128]{2,1,0:T(8,128)(2,1)}), bf16[16,480,128]{2,1,0:T(8,128)(2,1)}, u32[]{:S(2)}, u32[]{:S(2)}) async-start(bf16[16,480,128]{2,1,0:T(8,128)(2,1)} %copy-done.1), calls=%async_computation | async-start | bytes 3932160 | tf_op jit(solution)/shard_map/all_to_all | solution.py:240
  19.5 0.0 all-gather.6.cloned.1.call-start
  19.5 0.7 all-gather.6.cloned.1.call-update
  20.2 1.5 collective-permute-start
  21.7 0.0 collective-permute-start.2
  21.7 2.9 %collective-permute-start.1 = (s32[10,4,4]{0,2,1:T(4,128)S(1)}, s32[10,4,4]{0,2,1:T(4,128)S(1)}, u32[]{:S(2)}, u32[]{:S(2)}) collective-permute-start(s32[10,4,4]{0,2,1:T(4,128)S(1)} %copy-done.9), channel_id=1, source_target_pairs={{0,8},{4,12},{8,0},{12,4},{1,9},{5,13},{9,1},{13,5},{2,10},{6,14},... | collective-permute-start | bytes 1928 | tf_op jit(solution)/shard_map/ppermute | solution.py:184
  24.7 0.1 pad_add_fusion.1.off_ref
  24.7 28.6 %collective-permute-done = s32[10,4,4]{0,2,1:T(4,128)S(1)} collective-permute-done((s32[10,4,4]{0,2,1:T(4,128)S(1)}, s32[10,4,4]{0,2,1:T(4,128)S(1)}, u32[]{:S(2)}, u32[]{:S(2)}) %collective-permute-start) | collective-permute-done | bytes 672 | tf_op jit(solution)/shard_map/ppermute | solution.py:184
  53.3 9.9 %collective-permute-done.2 = s32[10,4,4]{0,2,1:T(4,128)S(1)} collective-permute-done((s32[10,4,4]{0,2,1:T(4,128)S(1)}, s32[10,4,4]{0,2,1:T(4,128)S(1)}, u32[]{:S(2)}, u32[]{:S(2)}) %collective-permute-start.2) | collective-permute-done | bytes 672 | tf_op jit(solution)/shard_map/ppermute | solution.py:184
  63.3 0.0 collective-permute-done.1
  63.3 0.2 copy.13
  63.5 0.1 reshape.36.idx_ref
  63.6 1.4 all-to-all-done.packed_ref
  65.0 14.2 %attention_forward.1.attn_ref = bf16[2560,128]{1,0:T(8,128)(2,1)} custom-call(s32[2]{0:T(128)S(1)} %pad_add_fusion.1.off_ref, s32[640]{0:T(1024)S(1)} %reshape.36.idx_ref, bf16[16,480,128]{2,1,0:T(8,128)(2,1)} %all-to-all-done.packed_ref), custom_call_target="tpu_custom_call" | custom-call | flops 2684354560 | bytes 2621440 | tf_op jit(solution)/shard_map/attention_forward/pallas_call | solution.py:258
  79.2 4.5 %all-to-all-start.1 = ((bf16[4,640,128]{2,1,0:T(8,128)(2,1)}), bf16[4,640,128]{2,1,0:T(8,128)(2,1)S(1)}, u32[]{:S(2)}, u32[]{:S(2)}) async-start(bf16[4,640,128]{2,1,0:T(8,128)(2,1)} %bitcast.8), calls=%async_computation.1 | async-start | bytes 1310720 | tf_op jit(solution)/shard_map/all_to_all | solution.py:272
  83.7 4.4 %fusion.8 = bf16[4,640,128]{1,2,0:T(8,128)(2,1)} fusion(bf16[4,128,2048]{2,1,0:T(8,128)(2,1)S(1)} %bitcast.60, bf16[1,640,2048]{2,1,0:T(8,128)(2,1)} %all-gather.6.cloned.1.call-done), kind=kOutput, calls=%fused_computation.15 | convolution fusion | flops 1342504960 | bytes 5373952 | tf_op jit(solution)/shard_map/te,hde->htd/dot_general | solution.py:255
  88.1 8.9 %all-to-all-done.1 = bf16[4,640,128]{2,1,0:T(8,128)(2,1)S(1)} async-done(((bf16[4,640,128]{2,1,0:T(8,128)(2,1)}), bf16[4,640,128]{2,1,0:T(8,128)(2,1)S(1)}, u32[]{:S(2)}, u32[]{:S(2)}) %all-to-all-start.1) | async-done | bytes 655392 | tf_op jit(solution)/shard_map/all_to_all | solution.py:272
  97.0 3.6 %fusion = f32[4,128,2048]{2,1,0:T(8,128)S(1)} fusion(bf16[4,640,128]{2,1,0:T(8,128)(2,1)S(1)} %all-to-all-done.1, bf16[1,640,2048]{2,1,0:T(8,128)(2,1)} %all-gather.6.cloned.1.call-done), kind=kOutput, calls=%fused_computation.1 | convolution fusion | flops 1342177280 | bytes 7471104 | tf_op jit(solution)/shard_map/htd,te->hde/dot_general | solution.py:279
  100.6 0.0 copy-start.6
  100.6 2.0 copy-done.6
  102.6 1.1 dynamic-slice_convert_fusion
  103.7 0.0 collective-permute-start.3
  103.7 6.7 %all-to-all-start.2 = ((bf16[4,640,128]{1,2,0:T(8,128)(2,1)}), bf16[4,640,128]{1,2,0:T(8,128)(2,1)S(1)}, u32[]{:S(2)}, u32[]{:S(2)}) async-start(bf16[4,640,128]{1,2,0:T(8,128)(2,1)} %fusion.8), calls=%async_computation.2 | async-start | bytes 1310720 | tf_op jit(solution)/shard_map/all_to_all | solution.py:276
  110.4 1.5 convolution_bitcast_fusion
  112.0 1.2 dynamic-slice_bitcast_fusion
  113.2 1.4 fusion.13
  114.5 10.9 %all-to-all-done.2 = bf16[4,640,128]{1,2,0:T(8,128)(2,1)S(1)} async-done(((bf16[4,640,128]{1,2,0:T(8,128)(2,1)}), bf16[4,640,128]{1,2,0:T(8,128)(2,1)S(1)}, u32[]{:S(2)}, u32[]{:S(2)}) %all-to-all-start.2) | async-done | bytes 655392 | tf_op jit(solution)/shard_map/all_to_all | solution.py:276
  125.4 0.3 copy.14
  125.7 0.0 collective-permute-done.3
  125.7 2.2 convert_add_fusion
  127.9 0.8 dynamic-slice_bitcast_fusion.1
  128.8 0.9 fusion.17
  129.7 2.4 %collective-permute-start.7 = (bf16[64,2048]{1,0:T(8,128)(2,1)}, bf16[64,2048]{1,0:T(8,128)(2,1)}, u32[]{:S(2)}, u32[]{:S(2)}) collective-permute-start(bf16[64,2048]{1,0:T(8,128)(2,1)} %get-tuple-element.30), channel_id=1, source_target_pairs={{0,4},{4,0},{8,12},{12,8},{1,5},{5,1},{9,13},{13,9},{2,6},{6,2},{1... | collective-permute-start | bytes 786440 | tf_op jit(solution)/shard_map/ppermute | solution.py:184
  132.1 0.9 collective-permute-start.8
  133.0 0.6 collective-permute-start.9
  133.5 22.1 %attention_backward.1 = bf16[16,480,128]{2,1,0:T(8,128)(2,1)S(1)} custom-call(s32[2]{0:T(128)S(1)} %pad_add_fusion.1.off_ref, s32[640]{0:T(1024)S(1)} %reshape.36.idx_ref, bf16[16,480,128]{2,1,0:T(8,128)(2,1)} %all-to-all-done.packed_ref, bf16[2560,128]{1,0:T(8,128)(2,1)} %attention_forward.1.attn_ref, bf16[2560,128]{1,0:T(8,128)(2,1)S(1)} %bitcast.61), custom_call_target="tpu_custom_call" | custom-call | flops 6710886400 | bytes 5242880 | tf_op jit(solution)/shard_map/attention_backward/pallas_call | solution.py:296
  155.6 1.3 copy-done.2
  156.9 9.0 %all-to-all-start.3 = ((bf16[16,480,128]{2,1,0:T(8,128)(2,1)}), bf16[16,480,128]{2,1,0:T(8,128)(2,1)}, u32[]{:S(2)}, u32[]{:S(2)}) async-start(bf16[16,480,128]{2,1,0:T(8,128)(2,1)} %copy-done.2), calls=%async_computation.3 | async-start | bytes 3932160 | tf_op jit(solution)/shard_map/all_to_all | solution.py:323
  165.8 0.0 all-gather.4.cloned.1.call-start
  165.9 0.0 collective-permute-done.7
  165.9 0.0 collective-permute-done.8
  165.9 0.0 collective-permute-done.9
  165.9 2.1 multiply_convert_fusion
  168.0 0.0 all-gather.4.cloned.1.call-update
  168.0 1.5 collective-permute-start.4
  169.6 1.5 collective-permute-start.5
  171.0 0.6 collective-permute-start.6
  171.6 42.8 %all-gather.4.cloned.1.call-done = bf16[256,2048]{1,0:T(8,128)(2,1)} async-done(((bf16[64,2048]{1,0:T(8,128)(2,1)}), bf16[256,2048]{1,0:T(8,128)(2,1)}) %all-gather.4.cloned.1.call-update) | async-done | bytes 1048592 | tf_op jit(solution)/shard_map/all_gather | solution.py:314
  214.4 0.1 collective-permute-start.10
  214.5 0.0 collective-permute-done.4
  214.5 0.0 collective-permute-done.5
  214.5 0.0 collective-permute-done.6
  214.5 2.8 %fusion.14 = bf16[1,160,2048]{2,1,0:T(8,128)(2,1)} fusion(bf16[160,2048]{1,0:T(8,128)(2,1)} %collective-permute-done.6, bf16[160,2048]{1,0:T(8,128)(2,1)} %collective-permute-done.5, f32[160,2048]{1,0:T(8,128)S(1)} %copy-done.7, bf16[160,2048]{1,0:T(8,128)(2,1)} %collective-permute-done.4), kind=kLoop, calls=%fused_computation.19 | loop fusion | flops 2293760 | bytes 3932160 | tf_op jit(solution)/shard_map/broadcast_in_dim | solution.py:332
  217.3 0.1 collective-permute-done.10
  217.4 4.2 %fusion.4 = f32[512,2048]{1,0:T(8,128)} fusion(bf16[256,2048]{1,0:T(8,128)(2,1)} %collective-permute-done.10, bf16[256,2048]{1,0:T(8,128)(2,1)S(1)} %copy-done.8, pred[]{:T(512)S(6)} %eq.3), kind=kLoop, calls=%fused_computation.6 | loop fusion | flops 10485760 | bytes 6291457 | tf_op jit(solution)/shard_map/convert_element_type | solution.py:318
  221.7 4.1 %all-to-all-done.3.in_ref = bf16[16,480,128]{2,1,0:T(8,128)(2,1)} async-done(((bf16[16,480,128]{2,1,0:T(8,128)(2,1)}), bf16[16,480,128]{2,1,0:T(8,128)(2,1)}, u32[]{:S(2)}, u32[]{:S(2)}) %all-to-all-start.3) | async-done | bytes 1966112 | tf_op jit(solution)/shard_map/all_to_all | solution.py:323
  225.8 3.4 %unpack_heads.1 = (bf16[160,2048]{1,0:T(8,128)(2,1)}, bf16[160,2048]{1,0:T(8,128)(2,1)}, bf16[160,2048]{1,0:T(8,128)(2,1)}) custom-call(bf16[16,480,128]{2,1,0:T(8,128)(2,1)} %all-to-all-done.3.in_ref), custom_call_target="tpu_custom_call" | custom-call | tf_op jit(solution)/shard_map/unpack_heads/pallas_call | solution.py:324
  (13 shorter events, 0.0 us)
Async XLA Ops:
  7.2 76.5 %copy-start = (bf16[512,2048]{1,0:T(8,128)(2,1)S(1)}, bf16[512,2048]{1,0:T(8,128)(2,1)}, u32[]{:S(2)}) copy-start(bf16[512,2048]{1,0:T(8,128)(2,1)} %param.10) | copy-start | bytes 6291460
  7.2 1.2 copy-start.3
  8.4 1.1 copy-start.4
  9.5 1.1 copy-start.5
  10.9 1.3 copy-start.1
  12.2 8.0 %copy-start.9 = (s32[10,4,4]{0,2,1:T(4,128)S(1)}, s32[10,4,4]{0,2,1:T(4,128)}, u32[]{:S(2)}) copy-start(s32[10,4,4]{0,2,1:T(4,128)} %param.9) | copy-start | bytes 1924
  12.2 52.8 %all-to-all-start = ((bf16[16,480,128]{2,1,0:T(8,128)(2,1)}), bf16[16,480,128]{2,1,0:T(8,128)(2,1)}, u32[]{:S(2)}, u32[]{:S(2)}) async-start(bf16[16,480,128]{2,1,0:T(8,128)(2,1)} %copy-done.1), calls=%async_computation | async-start | bytes 3932160 | tf_op jit(solution)/shard_map/all_to_all | solution.py:240
  19.5 64.2 %all-gather.6.cloned.1.call-start = ((), (), s32[]{:S(2)}) async-start(), calls=%async_computation.5 | async-start | bytes 3276800 | tf_op jit(solution)/shard_map/all_gather | solution.py:253
  20.2 33.1 %collective-permute-start = (s32[10,4,4]{0,2,1:T(4,128)S(1)}, s32[10,4,4]{0,2,1:T(4,128)S(1)}, u32[]{:S(2)}, u32[]{:S(2)}) collective-permute-start(s32[10,4,4]{0,2,1:T(4,128)S(1)} %copy-done.9), channel_id=1, source_target_pairs={{0,4},{4,0},{8,12},{12,8},{1,5},{5,1},{9,13},{13,9},{2,6},{6,2},{1... | collective-permute-start | bytes 1928 | tf_op jit(solution)/shard_map/ppermute | solution.py:184
  21.7 41.5 %collective-permute-start.2 = (s32[10,4,4]{0,2,1:T(4,128)S(1)}, s32[10,4,4]{0,2,1:T(4,128)S(1)}, u32[]{:S(2)}, u32[]{:S(2)}) collective-permute-start(s32[10,4,4]{0,2,1:T(4,128)S(1)} %copy-done.9), channel_id=1, source_target_pairs={{0,12},{4,8},{8,4},{12,0},{1,13},{5,9},{9,5},{13,1},{2,14},{6,10},... | collective-permute-start | bytes 1928 | tf_op jit(solution)/shard_map/ppermute | solution.py:184
  21.7 41.5 %collective-permute-start.1 = (s32[10,4,4]{0,2,1:T(4,128)S(1)}, s32[10,4,4]{0,2,1:T(4,128)S(1)}, u32[]{:S(2)}, u32[]{:S(2)}) collective-permute-start(s32[10,4,4]{0,2,1:T(4,128)S(1)} %copy-done.9), channel_id=1, source_target_pairs={{0,8},{4,12},{8,0},{12,4},{1,9},{5,13},{9,1},{13,5},{2,10},{6,14},... | collective-permute-start | bytes 1928 | tf_op jit(solution)/shard_map/ppermute | solution.py:184
  79.2 17.7 %all-to-all-start.1 = ((bf16[4,640,128]{2,1,0:T(8,128)(2,1)}), bf16[4,640,128]{2,1,0:T(8,128)(2,1)S(1)}, u32[]{:S(2)}, u32[]{:S(2)}) async-start(bf16[4,640,128]{2,1,0:T(8,128)(2,1)} %bitcast.8), calls=%async_computation.1 | async-start | bytes 1310720 | tf_op jit(solution)/shard_map/all_to_all | solution.py:272
  100.6 2.0 copy-start.6
  103.7 22.1 %collective-permute-start.3 = (bf16[256,2048]{1,0:T(8,128)(2,1)}, bf16[256,2048]{1,0:T(8,128)(2,1)}, u32[]{:S(2)}, u32[]{:S(2)}) collective-permute-start(bf16[256,2048]{1,0:T(8,128)(2,1)} %dynamic-slice_convert_fusion), channel_id=1, source_target_pairs={{0,16},{16,0},{1,17},{17,1},{2,18},{18,2},{3,19},{19,3},{4,20},{20... | collective-permute-start | bytes 3145736 | tf_op jit(solution)/shard_map/ppermute | solution.py:287
  103.7 21.7 %all-to-all-start.2 = ((bf16[4,640,128]{1,2,0:T(8,128)(2,1)}), bf16[4,640,128]{1,2,0:T(8,128)(2,1)S(1)}, u32[]{:S(2)}, u32[]{:S(2)}) async-start(bf16[4,640,128]{1,2,0:T(8,128)(2,1)} %fusion.8), calls=%async_computation.2 | async-start | bytes 1310720 | tf_op jit(solution)/shard_map/all_to_all | solution.py:276
  129.7 36.2 %collective-permute-start.7 = (bf16[64,2048]{1,0:T(8,128)(2,1)}, bf16[64,2048]{1,0:T(8,128)(2,1)}, u32[]{:S(2)}, u32[]{:S(2)}) collective-permute-start(bf16[64,2048]{1,0:T(8,128)(2,1)} %get-tuple-element.30), channel_id=1, source_target_pairs={{0,4},{4,0},{8,12},{12,8},{1,5},{5,1},{9,13},{13,9},{2,6},{6,2},{1... | collective-permute-start | bytes 786440 | tf_op jit(solution)/shard_map/ppermute | solution.py:184
  132.1 33.8 %collective-permute-start.8 = (bf16[64,2048]{1,0:T(8,128)(2,1)}, bf16[64,2048]{1,0:T(8,128)(2,1)}, u32[]{:S(2)}, u32[]{:S(2)}) collective-permute-start(bf16[64,2048]{1,0:T(8,128)(2,1)} %get-tuple-element.31), channel_id=1, source_target_pairs={{0,8},{4,12},{8,0},{12,4},{1,9},{5,13},{9,1},{13,5},{2,10},{6,14},... | collective-permute-start | bytes 786440 | tf_op jit(solution)/shard_map/ppermute | solution.py:184
  133.0 32.9 %collective-permute-start.9 = (bf16[64,2048]{1,0:T(8,128)(2,1)}, bf16[64,2048]{1,0:T(8,128)(2,1)}, u32[]{:S(2)}, u32[]{:S(2)}) collective-permute-start(bf16[64,2048]{1,0:T(8,128)(2,1)} %get-tuple-element.32), channel_id=1, source_target_pairs={{0,12},{4,8},{8,4},{12,0},{1,13},{5,9},{9,5},{13,1},{2,14},{6,10},... | collective-permute-start | bytes 786440 | tf_op jit(solution)/shard_map/ppermute | solution.py:184
  155.6 1.3 copy-start.2
  156.9 57.6 %copy-start.7 = (f32[160,2048]{1,0:T(8,128)S(1)}, f32[160,2048]{1,0:T(8,128)}, u32[]{:S(2)}) copy-start(f32[160,2048]{1,0:T(8,128)} %dynamic-slice_bitcast_fusion) | copy-start | bytes 3932164
  156.9 68.9 %all-to-all-start.3 = ((bf16[16,480,128]{2,1,0:T(8,128)(2,1)}), bf16[16,480,128]{2,1,0:T(8,128)(2,1)}, u32[]{:S(2)}, u32[]{:S(2)}) async-start(bf16[16,480,128]{2,1,0:T(8,128)(2,1)} %copy-done.2), calls=%async_computation.3 | async-start | bytes 3932160 | tf_op jit(solution)/shard_map/all_to_all | solution.py:323
  165.8 48.6 %all-gather.4.cloned.1.call-start = ((), (), s32[]{:S(2)}) async-start(), calls=%async_computation.4 | async-start | bytes 1310720 | tf_op jit(solution)/shard_map/all_gather | solution.py:314
  168.0 46.5 %collective-permute-start.4 = (bf16[160,2048]{1,0:T(8,128)(2,1)}, bf16[160,2048]{1,0:T(8,128)(2,1)}, u32[]{:S(2)}, u32[]{:S(2)}) collective-permute-start(bf16[160,2048]{1,0:T(8,128)(2,1)} %get-tuple-element.22), channel_id=1, source_target_pairs={{0,1},{1,0},{2,3},{3,2},{4,5},{5,4},{6,7},{7,6},{8,9},{9,8},{10,11... | collective-permute-start | bytes 1966088 | tf_op jit(solution)/shard_map/ppermute | solution.py:184
  169.6 44.9 %collective-permute-start.5 = (bf16[160,2048]{1,0:T(8,128)(2,1)}, bf16[160,2048]{1,0:T(8,128)(2,1)}, u32[]{:S(2)}, u32[]{:S(2)}) collective-permute-start(bf16[160,2048]{1,0:T(8,128)(2,1)} %get-tuple-element.23), channel_id=1, source_target_pairs={{0,2},{1,3},{2,0},{3,1},{4,6},{5,7},{6,4},{7,5},{8,10},{9,11},{10,... | collective-permute-start | bytes 1966088 | tf_op jit(solution)/shard_map/ppermute | solution.py:184
  171.0 43.5 %collective-permute-start.6 = (bf16[160,2048]{1,0:T(8,128)(2,1)}, bf16[160,2048]{1,0:T(8,128)(2,1)}, u32[]{:S(2)}, u32[]{:S(2)}) collective-permute-start(bf16[160,2048]{1,0:T(8,128)(2,1)} %get-tuple-element.24), channel_id=1, source_target_pairs={{0,3},{1,2},{2,1},{3,0},{4,7},{5,6},{6,5},{7,4},{8,11},{9,10},{10,... | collective-permute-start | bytes 1966088 | tf_op jit(solution)/shard_map/ppermute | solution.py:184
  214.4 3.0 %collective-permute-start.10 = (bf16[256,2048]{1,0:T(8,128)(2,1)}, bf16[256,2048]{1,0:T(8,128)(2,1)}, u32[]{:S(2)}, u32[]{:S(2)}) collective-permute-start(bf16[256,2048]{1,0:T(8,128)(2,1)} %all-gather.4.cloned.1.call-done), channel_id=1, source_target_pairs={{0,16},{16,0},{1,17},{17,1},{2,18},{18,2},{3,19},{19,3},{4,20},{20... | collective-permute-start | bytes 3145736 | tf_op jit(solution)/shard_map/ppermute | solution.py:315
  214.5 2.9 %copy-start.8 = (bf16[256,2048]{1,0:T(8,128)(2,1)S(1)}, bf16[256,2048]{1,0:T(8,128)(2,1)}, u32[]{:S(2)}) copy-start(bf16[256,2048]{1,0:T(8,128)(2,1)} %all-gather.4.cloned.1.call-done) | copy-start | bytes 3145732
Sparse Core Ops, SparseCore 0:
  22.1 51.3 all-gather.5
  168.8 45.5 all-gather.3
